TPU v7x, 256 devices: a whole 4x4x8 slice. The times are simulated.
256 devices in a mesh: ell: 32 (over y, x, core), rad: 8 (over z).
Axes of the slice: x: 4, y: 4, z: 8, core: 2. Of those that a mesh axis runs over, the one named last changes fastest.
Arguments:
- coefficients: bfloat16 [2, 256, 768, 1537], P(None, 'rad', 'ell'), may hold values from -0.14941406 to 0.14941406
- legendre: bfloat16 [32, 768, 1537], P(None, 'ell'), may hold values from -0.15625 to 0.15625
- bessel: bfloat16 [2, 32, 256, 1536], P(None, None, 'rad', 'ell'), may hold values from -0.375 to 0.375
- mode_counts: int32 [1536], replicated, may hold values from 1 to 256, as said below
Outputs:
- density: float32 [32, 64, 2048], P('rad', 'ell')
- displacement: float32 [32, 64, 2048], P('rad', 'ell')
Inputs may be any that keep to these rules, and one draw needn't show every extreme that they name: mode_counts[0] is 256.
All inputs are finite; a program needn't handle non-finite values.
Results may differ from a plain program's by a relative error of at most 0.0029.
Values may be sent and summed in bfloat16 or wider, within the bound.
No kernel may reach another device: no remote copies, remote signals or barrier semaphores. Data moves between devices by JAX's collectives and lax.ppermute only.
A program may use at most 256 MiB of HBM per device.

v0:
```python
import functools
import math

import jax
import jax.numpy as jnp
import numpy as np
from jax import lax
from jax.experimental import pallas as pl
from jax.experimental.pallas import tpu as pltpu
from jax.sharding import PartitionSpec as P

L = 1536
HALF_PIX = 1024
PAIR_DEV = 24
MODES_DEV = 32
STEPS = 14
GROUPS = 32
SPAN = STEPS * GROUPS
KPAD = 512
BF = jnp.bfloat16
F32 = jnp.float32


def step_info(k, e):
    p0 = PAIR_DEV * e
    n_low = 12 - p0 // 128
    first_high = (L - PAIR_DEV - p0) // 128
    is_low = k < n_low
    high_block = k - n_low + first_high
    return p0, n_low, is_low, high_block


def window_low(k, e):
    _, _, is_low, high_block = step_info(k, e)
    return jnp.where(is_low, jnp.maximum(k - 1, 0), jnp.minimum(high_block, 11))


def window_high(k, e):
    _, _, is_low, high_block = step_info(k, e)
    return jnp.where(is_low, k, jnp.minimum(high_block, 11) + 1)


def butterfly(parts, lane):
    parts = list(parts)
    for bit in range(5):
        distance = 4 << bit
        upper = (lane & distance) != 0
        for low in range(32):
            if low & (1 << bit):
                continue
            high = low | (1 << bit)
            first, second = parts[low], parts[high]
            parts[low] = jnp.where(upper, pltpu.roll(second, distance, 1), first)
            parts[high] = jnp.where(upper, second, pltpu.roll(first, 128 - distance, 1))
    return parts


def coeff_kernel(e_ref, first_ref, second_ref, out_ref, stage):
    k = pl.program_id(0)
    _, _, is_low, _ = step_info(k, e_ref[0])
    lane = lax.broadcasted_iota(jnp.int32, (8, 128), 1)
    row = lax.broadcasted_iota(jnp.int32, (8, 128), 0)

    def run(shifted):
        def part(c, carry):
            for tile in range(3):
                parts = []
                for n in range(MODES_DEV):
                    a = first_ref[c, n].astype(F32)[8 * tile : 8 * tile + 8]
                    b = second_ref[c, n].astype(F32)[8 * tile : 8 * tile + 8]
                    parts.append(shifted(a, b, tile))
                parts = butterfly(parts, lane)
                for g in range(GROUPS):
                    at = pl.multiple_of(c * PAIR_DEV + 8 * tile, 8)
                    stage[g, pl.ds(at, 8), :] = parts[g]
            return carry

        lax.fori_loop(0, 2, part, 0)

    @pl.when(is_low)
    def _():
        def shifted(a, b, tile):
            a = pltpu.roll(a, 8 * tile, 1, stride=1, stride_axis=0)
            b = pltpu.roll(b, 8 * tile, 1, stride=1, stride_axis=0)
            return jnp.where(lane >= row + 8 * tile, b, a)

        run(shifted)

    @pl.when(jnp.logical_not(is_low))
    def _():
        def shifted(a, b, tile):
            return jnp.where(lane < 127, pltpu.roll(a, 127, 1), pltpu.roll(b, 127, 1))

        run(shifted)

    for g in range(GROUPS):
        out_ref[0, g] = stage[g].astype(BF)


def coeff_blocks(e, coefficients):
    block = (2, MODES_DEV, PAIR_DEV, 128)
    return pl.pallas_call(
        coeff_kernel,
        out_shape=jax.ShapeDtypeStruct((STEPS, GROUPS, 2 * PAIR_DEV, 128), BF),
        grid_spec=pltpu.PrefetchScalarGridSpec(
            num_scalar_prefetch=1,
            grid=(STEPS,),
            in_specs=[
                pl.BlockSpec(block, lambda k, s: (0, 0, 0, window_low(k, s[0]))),
                pl.BlockSpec(block, lambda k, s: (0, 0, 0, window_high(k, s[0]))),
            ],
            out_specs=pl.BlockSpec((1, GROUPS, 2 * PAIR_DEV, 128), lambda k, s: (k, 0, 0, 0)),
            scratch_shapes=[pltpu.VMEM((GROUPS, 2 * PAIR_DEV, 128), F32)],
        ),
        compiler_params=pltpu.CompilerParams(vmem_limit_bytes=48 * 2**20),
        name="coeff_blocks",
    )(e, coefficients, coefficients)


def angular_kernel(e_ref, first_ref, second_ref, pick_ref, out_ref, stage, wide):
    k = pl.program_id(0)
    e = e_ref[0]
    p0, _, is_low, high_block = step_info(k, e)
    quarter = k % 4
    lane = lax.broadcasted_iota(jnp.int32, (PAIR_DEV, 128), 1)
    row = lax.broadcasted_iota(jnp.int32, (PAIR_DEV, 128), 0)

    def run(shifted, keep):
        for r in range(32):
            value = shifted(first_ref[r].astype(F32), second_ref[r].astype(F32))
            value = jnp.where(keep, value, 0.0)
            stage[pl.ds(r, PAIR_DEV, stride=32), :] = value

    @pl.when(jnp.logical_and(is_low, k < STEPS))
    def _():
        def shifted(a, b):
            a = pltpu.roll(a, 0, 1, stride=1, stride_axis=0)
            b = pltpu.roll(b, 0, 1, stride=1, stride_axis=0)
            return jnp.where(lane >= row, b, a)

        offset = 128 * k + lane
        run(shifted, (offset >= row) & (offset < L - p0))

    @pl.when(jnp.logical_and(jnp.logical_not(is_low), k < STEPS))
    def _():
        def shifted(a, b):
            return jnp.where(lane < 127, pltpu.roll(a, 127, 1), pltpu.roll(b, 127, 1))

        degree = 128 * high_block + lane
        run(shifted, (degree >= L - 1 - p0 - row) & (degree < L))

    @pl.when(k >= STEPS)
    def _():
        stage[...] = jnp.zeros_like(stage)

    for q in range(4):
        @pl.when(quarter == q)
        def _():
            wide[:, 128 * q : 128 * q + 128] = stage[...].astype(BF)

    @pl.when(quarter == 3)
    def _():
        for j in range(4):
            picked = jnp.dot(
                wide[...], pick_ref[:, 128 * j : 128 * j + 128], preferred_element_type=F32
            )
            for i in range(PAIR_DEV):
                out_ref[i, 32 * j : 32 * j + 32, :] = picked[32 * i : 32 * i + 32].astype(BF)


def angular_blocks(e, legendre):
    block = (32, PAIR_DEV, 128)
    pick = np.zeros((512, 512), np.float32)
    for q in range(4):
        for g in range(32):
            for j in range(4):
                pick[128 * q + 4 * g + j, 128 * j + 32 * q + g] = 1.0
    return pl.pallas_call(
        angular_kernel,
        out_shape=jax.ShapeDtypeStruct((PAIR_DEV, 128, KPAD), BF),
        grid_spec=pltpu.PrefetchScalarGridSpec(
            num_scalar_prefetch=1,
            grid=(16,),
            in_specs=[
                pl.BlockSpec(block, lambda k, s: (0, 0, window_low(jnp.minimum(k, STEPS - 1), s[0]))),
                pl.BlockSpec(block, lambda k, s: (0, 0, window_high(jnp.minimum(k, STEPS - 1), s[0]))),
                pl.BlockSpec((512, 512), lambda k, s: (0, 0)),
            ],
            out_specs=pl.BlockSpec((PAIR_DEV, 128, 128), lambda k, s: (0, 0, k // 4)),
            scratch_shapes=[pltpu.VMEM((PAIR_DEV * 32, 128), F32), pltpu.VMEM((PAIR_DEV * 32, 512), BF)],
        ),
        compiler_params=pltpu.CompilerParams(vmem_limit_bytes=48 * 2**20),
        name="angular_blocks",
    )(e, legendre, legendre, jnp.asarray(pick, BF))


def sums_kernel(e_ref, twist_ref, coeff_ref, table_ref, angular_ref, out_ref, left, right, turned):
    k = pl.program_id(0)
    e = e_ref[0]
    p0, n_low, is_low, high_block = step_info(k, e)
    base = jnp.where(is_low, p0 // 4 + GROUPS * k, GROUPS * jnp.minimum(high_block, 11))
    lane = lax.broadcasted_iota(jnp.int32, (64, 128), 1)
    slots = [(lane & 3) == j for j in range(4)]

    def group(g, carry):
        table = table_ref[jnp.minimum(base + g, L // 4 - 1)]
        weights = jnp.concatenate(
            [jnp.where(slots[j], table, jnp.zeros_like(table)) for j in range(4)], axis=0
        )
        radial = lax.dot_general(
            coeff_ref[0, g], weights, (((1,), (1,)), ((), ())), preferred_element_type=F32
        )
        radial = radial.astype(BF).astype(F32)
        at = k * GROUPS + g
        left[pl.ds(at, 48, stride=SPAN), :] = radial[:, :128]
        right[pl.ds(at, 48, stride=SPAN), :] = radial[:, 128:]
        return carry

    lax.fori_loop(0, GROUPS, group, 0, unroll=4)

    @pl.when(k == STEPS - 1)
    def _():
        slot = lax.broadcasted_iota(jnp.int32, (64, SPAN), 1)
        low_slot = slot < GROUPS * n_low
        near = lax.broadcasted_iota(jnp.int32, (32, 128), 1) < 64
        even_row = (lax.broadcasted_iota(jnp.int32, (32, 128), 0) & 1) == 0

        def order(i, carry):
            first = angular_ref[i, 0:64, 0:SPAN]
            second = angular_ref[i, 64:128, 0:SPAN]
            zero = jnp.zeros_like(first)
            first = jnp.concatenate(
                [jnp.where(low_slot, first, zero), jnp.where(low_slot, zero, first)], axis=0
            )
            second = jnp.concatenate(
                [jnp.where(low_slot, second, zero), jnp.where(low_slot, zero, second)], axis=0
            )
            folded = [[None, None], [None, None]]
            for c in range(2):
                at = pl.multiple_of((c * PAIR_DEV + i) * SPAN, 8)
                one = jnp.dot(first, left[pl.ds(at, SPAN), :].astype(BF), preferred_element_type=F32)
                two = jnp.dot(second, right[pl.ds(at, SPAN), :].astype(BF), preferred_element_type=F32)
                both = one + two
                for seg in range(2):
                    total = jnp.where(near, both[64 * seg : 64 * seg + 32], both[64 * seg + 32 : 64 * seg + 64])
                    other = pltpu.roll(total, 64, 1)
                    sign = jnp.where((i + seg) % 2 == 0, 1.0, -1.0)
                    folded[c][seg] = jnp.where(near, total + other, (other - total) * sign)
            for seg in range(2):
                scale = twist_ref[2, seg * PAIR_DEV + i]
                cos = jnp.where(even_row, twist_ref[0, seg * PAIR_DEV + i], scale)
                sin = jnp.where(even_row, twist_ref[1, seg * PAIR_DEV + i], 0.0)
                real, imag = folded[0][seg], folded[1][seg]
                turned[pl.ds(seg * 48 + i, 32, stride=96), :] = real * cos + imag * sin
                turned[pl.ds(seg * 48 + PAIR_DEV + i, 32, stride=96), :] = imag * cos - real * sin
            return carry

        lax.fori_loop(0, PAIR_DEV, order, 0)

        def pair(q, carry):
            rows = [
                jnp.transpose(turned[pl.ds(pl.multiple_of((2 * q + d) * 96, 8), 96), :])
                for d in range(2)
            ]
            for owner in range(8):
                north = [x[8 * owner : 8 * owner + 8] for x in rows]
                south = [x[64 + 8 * owner : 72 + 8 * owner] for x in rows]
                out_ref[owner, q] = jnp.concatenate(north, axis=0).astype(BF)
                out_ref[owner, 31 - q] = jnp.concatenate(south[::-1], axis=0).astype(BF)
            return carry

        lax.fori_loop(0, 16, pair, 0)


def cycle_sums(e, twist, coeffs, table, angular):
    return pl.pallas_call(
        sums_kernel,
        out_shape=jax.ShapeDtypeStruct((8, 32, 16, 96), BF),
        grid_spec=pltpu.PrefetchScalarGridSpec(
            num_scalar_prefetch=2,
            grid=(STEPS,),
            in_specs=[
                pl.BlockSpec((1, GROUPS, 48, 128), lambda k, s, t: (k, 0, 0, 0)),
                pl.BlockSpec((L // 4, 64, 128), lambda k, s, t: (0, 0, 0), pipeline_mode=pl.Buffered(1)),
                pl.BlockSpec((PAIR_DEV, 128, KPAD), lambda k, s, t: (0, 0, 0), pipeline_mode=pl.Buffered(1)),
            ],
            out_specs=pl.BlockSpec((8, 32, 16, 96), lambda k, s, t: (0, 0, 0, 0)),
            scratch_shapes=[
                pltpu.VMEM((48 * SPAN, 128), F32),
                pltpu.VMEM((48 * SPAN, 128), F32),
                pltpu.VMEM((32 * 96, 128), F32),
            ],
        ),
        compiler_params=pltpu.CompilerParams(vmem_limit_bytes=56 * 2**20),
        name="cycle_sums",
    )(e, twist, coeffs, table, angular)


SOURCES_STEP = 8


def pixels_kernel(in_ref, basis_ref, dens_ref, disp_ref, total):
    step = pl.program_id(0)
    col = lax.broadcasted_iota(jnp.int32, (16, 96), 1)
    order = col % PAIR_DEV
    odd = (order + jnp.where(col >= 48, 1, 0)) % 2 == 1
    acc = None
    for source in range(SOURCES_STEP):
        value = in_ref[0, source].astype(F32)
        for radial in range(1, 8):
            value = value + in_ref[radial, source].astype(F32)
        top = value.astype(BF).astype(F32)
        rest = value - top
        rows = jnp.concatenate(
            [
                jnp.where(odd, 0.0, top),
                jnp.where(odd, top, 0.0),
                jnp.where(odd, 0.0, rest),
                jnp.where(odd, rest, 0.0),
            ],
            axis=0,
        ).astype(BF)
        part = jnp.dot(rows, basis_ref[source], preferred_element_type=F32)
        part = part[0:32] + part[32:64]
        acc = part if acc is None else acc + part

    @pl.when(step == 0)
    def _():
        total[...] = acc

    @pl.when(step > 0)
    def _():
        total[...] += acc

    @pl.when(step == pl.num_programs(0) - 1)
    def _():
        even, odd_part = total[0:16], total[16:32]
        near, far = even + odd_part, even - odd_part
        for cycle in range(2):
            for shell in range(4):
                at = cycle * 8 + shell
                for ref, row in ((dens_ref, at), (disp_ref, at + 4)):
                    ref[shell, cycle : cycle + 1, 0:HALF_PIX] = near[row : row + 1]
                    ref[shell, cycle : cycle + 1, HALF_PIX:] = far[row : row + 1]


def pixel_basis():
    source = np.arange(32)[:, None, None]
    i = np.arange(PAIR_DEV)[None, None, :]
    low = PAIR_DEV * source + i
    orders = np.concatenate([low, L - 1 - low], axis=1)
    phase = (orders[..., None] * (np.arange(HALF_PIX) + 1)) % 2048
    angle = 2.0 * math.pi / 2048 * phase
    basis = np.stack([np.cos(angle), -np.sin(angle)], axis=2)
    return basis.reshape(32, 96, HALF_PIX).astype(jnp.bfloat16)


def pixels(received):
    out = jax.ShapeDtypeStruct((4, 2, 2 * HALF_PIX), F32)
    spec = pl.BlockSpec((4, 2, 2 * HALF_PIX), lambda k: (0, 0, 0))
    return pl.pallas_call(
        pixels_kernel,
        out_shape=(out, out),
        grid=(32 // SOURCES_STEP,),
        in_specs=[
            pl.BlockSpec((8, SOURCES_STEP, 16, 96), lambda k: (0, k, 0, 0)),
            pl.BlockSpec((SOURCES_STEP, 96, HALF_PIX), lambda k: (k, 0, 0)),
        ],
        out_specs=(spec, spec),
        scratch_shapes=[pltpu.VMEM((32, HALF_PIX), F32)],
        compiler_params=pltpu.CompilerParams(vmem_limit_bytes=48 * 2**20),
        name="pixels",
    )(received, jnp.asarray(pixel_basis()))


def radial_table(bessel, mode_counts):
    width = bessel.shape[3]
    counts = lax.dynamic_slice_in_dim(mode_counts, lax.axis_index("ell") * width, width)
    modes = lax.axis_index("rad") * MODES_DEV + jnp.arange(MODES_DEV, dtype=jnp.int32)
    live = modes[:, None] < counts[None, :]
    table = jnp.where(live, bessel, jnp.zeros_like(bessel))
    table = table.reshape(2, 8, 4, MODES_DEV, width // 4, 4)
    table = table.transpose(4, 1, 0, 2, 3, 5)
    return table.reshape(width // 4, 64, 4 * MODES_DEV)


def twist_table():
    low = np.arange(L // 2).reshape(32, PAIR_DEV)
    orders = np.concatenate([low, L - 1 - low], axis=1)
    weight = np.where(orders == 0, 1.0, 2.0)
    angle = 2.0 * math.pi / 4096 * orders
    return np.stack([weight * np.cos(angle), weight * np.sin(angle), weight], axis=1).astype(np.float32)


def local(coefficients, legendre, bessel, mode_counts):
    e = lax.axis_index("ell")
    e_arr = e.reshape(1).astype(jnp.int32)
    twist = lax.dynamic_index_in_dim(jnp.asarray(twist_table()), e, 0, keepdims=False)
    table = lax.all_gather(radial_table(bessel, mode_counts), "ell", axis=0, tiled=True)
    coeffs = coeff_blocks(e_arr, coefficients)
    angular = angular_blocks(e_arr, legendre)
    sums = cycle_sums(e_arr, twist, coeffs, table, angular)
    received = lax.all_to_all(
        sums.reshape(256, 16, 96), ("rad", "ell"), split_axis=0, concat_axis=0, tiled=True
    )
    return pixels(received.reshape(8, 32, 16, 96))


def solution(mesh):
    in_specs = (P(None, "rad", "ell", None), P(None, "ell", None), P(None, None, "rad", "ell"), P())
    out_specs = (P("rad", "ell", None), P("rad", "ell", None))
    return jax.shard_map(local, mesh=mesh, in_specs=in_specs, out_specs=out_specs, check_vma=False)
```

profile of v0, /device:TPU:1, one launch (start us, length us, event | category | flops | bytes accessed | tf_op | source)
XLA Modules:
  0.0 180.1 jit_solution(6569493652050466292)
XLA Ops:
  7.2 0.0 all-gather.2.cloned.1.call-start
  7.2 1.4 copy.13
  8.6 0.8 dynamic_slice.8
  9.4 0.1 broadcast_compare_fusion
  9.5 0.1 broadcast_select_fusion
  9.6 2.1 %copy.14 = bf16[12,8,2,4,32,4]{0,5,4,3,2,1:T(4,128)(2,1)S(1)} copy(bf16[12,8,2,4,32,4]{4,5,0,3,1,2:T(4,128)(2,1)S(1)} %bitcast.12) | data formatting | bytes 393216 | tf_op jit(solution)/shard_map/transpose | solution.py:383
  11.7 1.6 copy.15
  13.3 0.0 all-gather.2.cloned.1.call-update
  13.3 0.0 copy-start
  13.4 2.4 %copy-done = bf16[2,32,24,1537]{3,2,1,0:T(8,128)(2,1)S(1)} copy-done((bf16[2,32,24,1537]{3,2,1,0:T(8,128)(2,1)S(1)}, bf16[2,32,24,1537]{3,2,1,0:T(8,128)(2,1)}, u32[]{:S(2)}) %copy-start) | copy-done | bytes 4721688
  15.8 0.0 copy-start.1
  15.8 0.0 copy-start.2
  15.8 25.9 %coeff_blocks.1.coeff_ref = bf16[14,32,48,128]{3,2,1,0:T(8,128)(2,1)} custom-call(s32[1]{0:T(128)} %bitcast.e_ref, bf16[2,32,24,1537]{3,2,1,0:T(8,128)(2,1)S(1)} %copy-done, bf16[2,32,24,1537]{3,2,1,0:T(8,128)(2,1)S(1)} %copy-done), custom_call_target="tpu_custom_call" | custom-call | tf_op jit(solution)/shard_map/coeff_blocks/pallas_call | solution.py:102
  41.7 0.0 copy-done.1
  41.7 0.0 copy-done.2
  41.8 14.3 %angular_blocks.1.angular_ref = bf16[24,128,512]{2,1,0:T(8,128)(2,1)} custom-call(s32[1]{0:T(128)} %bitcast.e_ref, bf16[32,24,1537]{2,1,0:T(8,128)(2,1)S(1)} %copy-done.1, bf16[32,24,1537]{2,1,0:T(8,128)(2,1)S(1)} %copy-done.1, bf16[512,512]{1,0:T(8,128)(2,1)S(1)} %copy-done.2), custom_call_target="tpu_custom_call" | custom-call | tf_op jit(solution)/shard_map/angular_blocks/pallas_call | solution.py:178
  56.1 1.3 dynamic-slice_bitcast_fusion.twist_ref
  57.3 14.5 %all-gather.2.cloned.1.call-done.table_ref = bf16[384,64,128]{2,1,0:T(8,128)(2,1)} async-done(((bf16[12,64,128]{2,1,0:T(8,128)(2,1)}), bf16[384,64,128]{2,1,0:T(8,128)(2,1)}) %all-gather.2.cloned.1.call-update) | async-done | bytes 6291472 | tf_op jit(solution)/shard_map/all_gather | solution.py:399
  71.9 55.3 %cycle_sums.1 = bf16[8,32,16,96]{3,2,1,0:T(8,128)(2,1)} custom-call(s32[1]{0:T(128)} %bitcast.e_ref, f32[3,48]{1,0:T(4,128)} %dynamic-slice_bitcast_fusion.twist_ref, bf16[14,32,48,128]{3,2,1,0:T(8,128)(2,1)} %coeff_blocks.1.coeff_ref, bf16[384,64,128]{2,1,0:T(8,128)(2,1)} %all-gather.2.cloned.1.call-done.table_ref, ...), custom_call_target="tpu_custom_call" | custom-call | tf_op jit(solution)/shard_map/cycle_sums/pallas_call | solution.py:276
  127.2 41.0 %all_to_all.5 = bf16[256,16,96]{2,1,0:T(8,128)(2,1)S(1)} all-to-all(bf16[256,16,96]{2,1,0:T(8,128)(2,1)} %bitcast.11), channel_id=1, replica_groups=mesh['ell'=32,'rad'=8] {'rad','ell'}, dimensions={0} | all-to-all | bytes 1572864 | tf_op jit(solution)/shard_map/all_to_all | solution.py:403
  168.2 5.0 %pixels.1 = (f32[4,2,2048]{2,1,0:T(2,128)}, f32[4,2,2048]{2,1,0:T(2,128)}) custom-call(bf16[8,32,16,96]{3,2,1,0:T(8,128)(2,1)S(1)} %bitcast.9, bf16[32,96,1024]{2,1,0:T(8,128)(2,1)} %constant.31.clone.basis_ref), custom_call_target="tpu_custom_call" | custom-call | tf_op jit(solution)/shard_map/pixels/pallas_call | solution.py:361
  (1 shorter events, 0.0 us)
Async XLA Ops:
  7.2 64.7 %all-gather.2.cloned.1.call-start = ((), (), s32[]{:S(2)}) async-start(), calls=%async_computation.1 | async-start | bytes 6488064 | tf_op jit(solution)/shard_map/all_gather | solution.py:399
  13.3 2.5 %copy-start = (bf16[2,32,24,1537]{3,2,1,0:T(8,128)(2,1)S(1)}, bf16[2,32,24,1537]{3,2,1,0:T(8,128)(2,1)}, u32[]{:S(2)}) copy-start(bf16[2,32,24,1537]{3,2,1,0:T(8,128)(2,1)} %second_ref.2) | copy-start | bytes 14164996
  15.8 26.0 %copy-start.1 = (bf16[32,24,1537]{2,1,0:T(8,128)(2,1)S(1)}, bf16[32,24,1537]{2,1,0:T(8,128)(2,1)}, u32[]{:S(2)}) copy-start(bf16[32,24,1537]{2,1,0:T(8,128)(2,1)} %second_ref.3) | copy-start | bytes 7082500
  15.8 26.0 %copy-start.2 = (bf16[512,512]{1,0:T(8,128)(2,1)S(1)}, bf16[512,512]{1,0:T(8,128)(2,1)}, u32[]{:S(2)}) copy-start(bf16[512,512]{1,0:T(8,128)(2,1)} %constant.30.clone.pick_ref) | copy-start | bytes 1572868
Sparse Core Ops, SparseCore 0:
  13.5 58.3 all-gather.1
where the time goes:
time: 180 us
  Pallas kernels  101 us (56%)
  blocking collectives  41 us (23%)
  waiting for transfers between devices  14.6 us (8%)
  between operations  14.1 us (8%)
  local copies, waits for them, and re-layouts  9.65 us (5%)
    pallas_call x1, Pallas kernels, cycle_sums(): pl.pallas_call(sums_kernel, out_shape=jax.ShapeDtypeStruct((8, 32, 16, 96...  55.3 us
    all_to_all x1, blocking collectives, local(): lax.all_to_all(sums.reshape(256, 16, 96), ('rad', 'ell'), split_axis=0, c...  41 us
    pallas_call x1, Pallas kernels, coeff_blocks(): pl.pallas_call(coeff_kernel, out_shape=jax.ShapeDtypeStruct((STEPS, GROUP...  25.9 us
    all_gather x1, waiting for transfers between devices, local(): lax.all_gather(radial_table(bessel, mode_counts), 'ell', axis=0, tiled=True)  14.5 us
    pallas_call x1, Pallas kernels, angular_blocks(): pl.pallas_call(angular_kernel, out_shape=jax.ShapeDtypeStruct((PAIR_DEV,...  14.3 us
    pallas_call x1, Pallas kernels, pixels(): pl.pallas_call(pixels_kernel, out_shape=(out, out), grid=(32 // SOURCES_S...  5.02 us
    unnamed x7, local copies, waits for them, and re-layouts  3.85 us
  transfers between devices with their start and end apart: 1, of which 1 were waited for; matrix products, arithmetic and copies ran while one was open for 1% of the time, Pallas kernels for 22%

commit v1 on v0

--- a/solution.py
+++ b/solution.py
@@ -16,6 +16,7 @@
 STEPS = 14
 GROUPS = 32
 SPAN = STEPS * GROUPS
+PITCH = SPAN + 8
 KPAD = 512
 BF = jnp.bfloat16
 F32 = jnp.float32
@@ -194,16 +195,33 @@
     )(e, legendre, legendre, jnp.asarray(pick, BF))
 
 
-def sums_kernel(e_ref, twist_ref, coeff_ref, table_ref, angular_ref, out_ref, left, right, turned):
+def table_first(k, e):
+    p0, _, is_low, high_block = step_info(k, e)
+    return jnp.where(is_low, p0 // 4 + GROUPS * k, GROUPS * jnp.minimum(high_block, 11))
+
+
+def table_start(k, e):
+    return jnp.minimum(table_first(k, e), L // 4 - GROUPS)
+
+
+def sums_kernel(
+    e_ref, twist_ref, coeff_ref, table_ref, angular_hbm, out_ref, left, right, turned, angular_ref, sem
+):
     k = pl.program_id(0)
     e = e_ref[0]
-    p0, n_low, is_low, high_block = step_info(k, e)
-    base = jnp.where(is_low, p0 // 4 + GROUPS * k, GROUPS * jnp.minimum(high_block, 11))
+    _, n_low, _, _ = step_info(k, e)
+    base = table_first(k, e) - table_start(k, e)
+    fetch = pltpu.make_async_copy(angular_hbm, angular_ref, sem)
+
+    @pl.when(k == 0)
+    def _():
+        fetch.start()
+
     lane = lax.broadcasted_iota(jnp.int32, (64, 128), 1)
     slots = [(lane & 3) == j for j in range(4)]
 
     def group(g, carry):
-        table = table_ref[jnp.minimum(base + g, L // 4 - 1)]
+        table = table_ref[jnp.minimum(base + g, GROUPS - 1)]
         weights = jnp.concatenate(
             [jnp.where(slots[j], table, jnp.zeros_like(table)) for j in range(4)], axis=0
         )
@@ -212,14 +230,15 @@
         )
         radial = radial.astype(BF).astype(F32)
         at = k * GROUPS + g
-        left[pl.ds(at, 48, stride=SPAN), :] = radial[:, :128]
-        right[pl.ds(at, 48, stride=SPAN), :] = radial[:, 128:]
+        left[pl.ds(at, 48, stride=PITCH), :] = radial[:, :128]
+        right[pl.ds(at, 48, stride=PITCH), :] = radial[:, 128:]
         return carry
 
-    lax.fori_loop(0, GROUPS, group, 0, unroll=4)
+    lax.fori_loop(0, GROUPS, group, 0, unroll=True)
 
     @pl.when(k == STEPS - 1)
     def _():
+        fetch.wait()
         slot = lax.broadcasted_iota(jnp.int32, (64, SPAN), 1)
         low_slot = slot < GROUPS * n_low
         near = lax.broadcasted_iota(jnp.int32, (32, 128), 1) < 64
@@ -237,7 +256,7 @@
             )
             folded = [[None, None], [None, None]]
             for c in range(2):
-                at = pl.multiple_of((c * PAIR_DEV + i) * SPAN, 8)
+                at = pl.multiple_of((c * PAIR_DEV + i) * PITCH, 8)
                 one = jnp.dot(first, left[pl.ds(at, SPAN), :].astype(BF), preferred_element_type=F32)
                 two = jnp.dot(second, right[pl.ds(at, SPAN), :].astype(BF), preferred_element_type=F32)
                 both = one + two
@@ -255,7 +274,7 @@
                 turned[pl.ds(seg * 48 + PAIR_DEV + i, 32, stride=96), :] = imag * cos - real * sin
             return carry
 
-        lax.fori_loop(0, PAIR_DEV, order, 0)
+        lax.fori_loop(0, PAIR_DEV, order, 0, unroll=8)
 
         def pair(q, carry):
             rows = [
@@ -269,7 +288,7 @@
                 out_ref[owner, 31 - q] = jnp.concatenate(south[::-1], axis=0).astype(BF)
             return carry
 
-        lax.fori_loop(0, 16, pair, 0)
+        lax.fori_loop(0, 16, pair, 0, unroll=4)
 
 
 def cycle_sums(e, twist, coeffs, table, angular):
@@ -281,14 +300,19 @@
             grid=(STEPS,),
             in_specs=[
                 pl.BlockSpec((1, GROUPS, 48, 128), lambda k, s, t: (k, 0, 0, 0)),
-                pl.BlockSpec((L // 4, 64, 128), lambda k, s, t: (0, 0, 0), pipeline_mode=pl.Buffered(1)),
-                pl.BlockSpec((PAIR_DEV, 128, KPAD), lambda k, s, t: (0, 0, 0), pipeline_mode=pl.Buffered(1)),
+                pl.BlockSpec(
+                    (pl.Element(GROUPS), pl.Element(64), pl.Element(128)),
+                    lambda k, s, t: (table_start(k, s[0]), 0, 0),
+                ),
+                pl.BlockSpec(memory_space=pl.ANY),
             ],
             out_specs=pl.BlockSpec((8, 32, 16, 96), lambda k, s, t: (0, 0, 0, 0)),
             scratch_shapes=[
-                pltpu.VMEM((48 * SPAN, 128), F32),
-                pltpu.VMEM((48 * SPAN, 128), F32),
+                pltpu.VMEM((48 * PITCH, 128), F32),
+                pltpu.VMEM((48 * PITCH, 128), F32),
                 pltpu.VMEM((32 * 96, 128), F32),
+                pltpu.VMEM((PAIR_DEV, 128, KPAD), BF),
+                pltpu.SemaphoreType.DMA,
             ],
         ),
         compiler_params=pltpu.CompilerParams(vmem_limit_bytes=56 * 2**20),

time: 180 us -> 149 us (0.83)
  Pallas kernels: 101 us -> 68.5 us
    pallas_call x1, Pallas kernels: 55.3 us -> 23.2 us  [cycle_sums(): pl.pallas_call(sums_kernel, out_shape=jax.ShapeDtypeStruct((8, 32, 16, 96...]
  transfers between devices with their start and end apart: 1 -> 1, of which waited for: 1 -> 1; matrix products, arithmetic and copies ran while one was open for 1% -> 1% of each run, Pallas kernels for 22% -> 27%
where the time goes in v1:
time: 149 us; the launch traced here: 148 us
  Pallas kernels  68.5 us (46%)
  blocking collectives  41.1 us (28%)
  waiting for transfers between devices  14.6 us (10%)
  between operations  14.1 us (9%)
  local copies, waits for them, and re-layouts  9.65 us (6%)
    all_to_all x1, blocking collectives, local(): lax.all_to_all(sums.reshape(256, 16, 96), ('rad', 'ell'), split_axis=0, c...  41.1 us
    pallas_call x1, Pallas kernels, coeff_blocks(): pl.pallas_call(coeff_kernel, out_shape=jax.ShapeDtypeStruct((STEPS, GROUP...  25.9 us
    pallas_call x1, Pallas kernels, cycle_sums(): pl.pallas_call(sums_kernel, out_shape=jax.ShapeDtypeStruct((8, 32, 16, 96...  23.2 us
    all_gather x1, waiting for transfers between devices, local(): lax.all_gather(radial_table(bessel, mode_counts), 'ell', axis=0, tiled=True)  14.5 us
    pallas_call x1, Pallas kernels, angular_blocks(): pl.pallas_call(angular_kernel, out_shape=jax.ShapeDtypeStruct((PAIR_DEV,...  14.3 us
    pallas_call x1, Pallas kernels, pixels(): pl.pallas_call(pixels_kernel, out_shape=(out, out), grid=(32 // SOURCES_S...  5.03 us
    unnamed x7, local copies, waits for them, and re-layouts  3.85 us
  transfers between devices with their start and end apart: 1, of which 1 were waited for; matrix products, arithmetic and copies ran while one was open for 1% of the time, Pallas kernels for 27%

profile of v1, /device:TPU:1, one launch (start us, length us, event | category | flops | bytes accessed | tf_op | source)
XLA Modules:
  0.0 148.1 jit_solution(5047037368541775260)
XLA Ops:
  7.2 0.0 all-gather.2.cloned.1.call-start
  7.2 1.4 copy.13
  8.6 0.8 dynamic_slice.8
  9.4 0.1 broadcast_compare_fusion
  9.5 0.1 broadcast_select_fusion
  9.6 2.1 %copy.14 = bf16[12,8,2,4,32,4]{0,5,4,3,2,1:T(4,128)(2,1)S(1)} copy(bf16[12,8,2,4,32,4]{4,5,0,3,1,2:T(4,128)(2,1)S(1)} %bitcast.12) | data formatting | bytes 393216 | tf_op jit(solution)/shard_map/transpose | solution.py:407
  11.7 1.6 %copy.15 = bf16[12,64,128]{2,1,0:T(8,128)(2,1)} copy(bf16[12,64,128]{0,2,1:T(8,128)(2,1)S(1)} %bitcast.10) | data formatting | bytes 393216 | tf_op jit(solution)/shard_map/reshape | solution.py:408
  13.3 0.0 all-gather.2.cloned.1.call-update
  13.3 0.0 copy-start
  13.4 2.4 %copy-done = bf16[2,32,24,1537]{3,2,1,0:T(8,128)(2,1)S(1)} copy-done((bf16[2,32,24,1537]{3,2,1,0:T(8,128)(2,1)S(1)}, bf16[2,32,24,1537]{3,2,1,0:T(8,128)(2,1)}, u32[]{:S(2)}) %copy-start) | copy-done | bytes 4721688
  15.8 0.0 copy-start.1
  15.8 0.0 copy-start.2
  15.8 25.9 %coeff_blocks.1.coeff_ref = bf16[14,32,48,128]{3,2,1,0:T(8,128)(2,1)} custom-call(s32[1]{0:T(128)} %bitcast.e_ref, bf16[2,32,24,1537]{3,2,1,0:T(8,128)(2,1)S(1)} %copy-done, bf16[2,32,24,1537]{3,2,1,0:T(8,128)(2,1)S(1)} %copy-done), custom_call_target="tpu_custom_call" | custom-call | tf_op jit(solution)/shard_map/coeff_blocks/pallas_call | solution.py:103
  41.7 0.0 copy-done.1
  41.7 0.0 copy-done.2
  41.8 14.3 %angular_blocks.1.angular_hbm = bf16[24,128,512]{2,1,0:T(8,128)(2,1)} custom-call(s32[1]{0:T(128)} %bitcast.e_ref, bf16[32,24,1537]{2,1,0:T(8,128)(2,1)S(1)} %copy-done.1, bf16[32,24,1537]{2,1,0:T(8,128)(2,1)S(1)} %copy-done.1, bf16[512,512]{1,0:T(8,128)(2,1)S(1)} %copy-done.2), custom_call_target="tpu_custom_call" | custom-call | tf_op jit(solution)/shard_map/angular_blocks/pallas_call | solution.py:179
  56.1 1.3 dynamic-slice_bitcast_fusion.twist_ref
  57.3 14.5 %all-gather.2.cloned.1.call-done.table_ref = bf16[384,64,128]{2,1,0:T(8,128)(2,1)} async-done(((bf16[12,64,128]{2,1,0:T(8,128)(2,1)}), bf16[384,64,128]{2,1,0:T(8,128)(2,1)}) %all-gather.2.cloned.1.call-update) | async-done | bytes 6291472 | tf_op jit(solution)/shard_map/all_gather | solution.py:423
  71.9 23.2 %cycle_sums.1 = bf16[8,32,16,96]{3,2,1,0:T(8,128)(2,1)} custom-call(s32[1]{0:T(128)} %bitcast.e_ref, f32[3,48]{1,0:T(4,128)} %dynamic-slice_bitcast_fusion.twist_ref, bf16[14,32,48,128]{3,2,1,0:T(8,128)(2,1)} %coeff_blocks.1.coeff_ref, bf16[384,64,128]{2,1,0:T(8,128)(2,1)} %all-gather.2.cloned.1.call-done.table_ref, ...), custom_call_target="tpu_custom_call" | custom-call | tf_op jit(solution)/shard_map/cycle_sums/pallas_call | solution.py:295
  95.1 41.1 %all_to_all.5 = bf16[256,16,96]{2,1,0:T(8,128)(2,1)S(1)} all-to-all(bf16[256,16,96]{2,1,0:T(8,128)(2,1)} %bitcast.11), channel_id=1, replica_groups=mesh['ell'=32,'rad'=8] {'rad','ell'}, dimensions={0} | all-to-all | bytes 1572864 | tf_op jit(solution)/shard_map/all_to_all | solution.py:427
  136.2 5.0 %pixels.1 = (f32[4,2,2048]{2,1,0:T(2,128)}, f32[4,2,2048]{2,1,0:T(2,128)}) custom-call(bf16[8,32,16,96]{3,2,1,0:T(8,128)(2,1)S(1)} %bitcast.9, bf16[32,96,1024]{2,1,0:T(8,128)(2,1)} %constant.31.clone.basis_ref), custom_call_target="tpu_custom_call" | custom-call | tf_op jit(solution)/shard_map/pixels/pallas_call | solution.py:385
  (1 shorter events, 0.0 us)
Async XLA Ops:
  7.2 64.7 %all-gather.2.cloned.1.call-start = ((), (), s32[]{:S(2)}) async-start(), calls=%async_computation.1 | async-start | bytes 6488064 | tf_op jit(solution)/shard_map/all_gather | solution.py:423
  13.3 2.5 %copy-start = (bf16[2,32,24,1537]{3,2,1,0:T(8,128)(2,1)S(1)}, bf16[2,32,24,1537]{3,2,1,0:T(8,128)(2,1)}, u32[]{:S(2)}) copy-start(bf16[2,32,24,1537]{3,2,1,0:T(8,128)(2,1)} %second_ref.2) | copy-start | bytes 14164996
  15.8 26.0 %copy-start.1 = (bf16[32,24,1537]{2,1,0:T(8,128)(2,1)S(1)}, bf16[32,24,1537]{2,1,0:T(8,128)(2,1)}, u32[]{:S(2)}) copy-start(bf16[32,24,1537]{2,1,0:T(8,128)(2,1)} %second_ref.3) | copy-start | bytes 7082500
  15.8 26.0 %copy-start.2 = (bf16[512,512]{1,0:T(8,128)(2,1)S(1)}, bf16[512,512]{1,0:T(8,128)(2,1)}, u32[]{:S(2)}) copy-start(bf16[512,512]{1,0:T(8,128)(2,1)} %constant.30.clone.pick_ref) | copy-start | bytes 1572868
Sparse Core Ops, SparseCore 0:
  13.5 58.3 all-gather.1

commit v2 on v1

--- a/solution.py
+++ b/solution.py
@@ -18,6 +18,9 @@
 SPAN = STEPS * GROUPS
 PITCH = SPAN + 8
 KPAD = 512
+ROW_PITCH = 40
+PIECE = 12
+SHIFTS = (0, 1, -1, 2)
 BF = jnp.bfloat16
 F32 = jnp.float32
 
@@ -56,46 +59,42 @@
     return parts
 
 
-def coeff_kernel(e_ref, first_ref, second_ref, out_ref, stage):
+def coeff_kernel(e_ref, first_ref, second_ref, out_ref):
     k = pl.program_id(0)
     _, _, is_low, _ = step_info(k, e_ref[0])
-    lane = lax.broadcasted_iota(jnp.int32, (8, 128), 1)
-    row = lax.broadcasted_iota(jnp.int32, (8, 128), 0)
+    lane8 = lax.broadcasted_iota(jnp.int32, (8, 128), 1)
+    row8 = lax.broadcasted_iota(jnp.int32, (8, 128), 0)
+    lane = lax.broadcasted_iota(jnp.int32, (16, 128), 1)
 
     def run(shifted):
-        def part(c, carry):
-            for tile in range(3):
-                parts = []
-                for n in range(MODES_DEV):
-                    a = first_ref[c, n].astype(F32)[8 * tile : 8 * tile + 8]
-                    b = second_ref[c, n].astype(F32)[8 * tile : 8 * tile + 8]
-                    parts.append(shifted(a, b, tile))
-                parts = butterfly(parts, lane)
-                for g in range(GROUPS):
-                    at = pl.multiple_of(c * PAIR_DEV + 8 * tile, 8)
-                    stage[g, pl.ds(at, 8), :] = parts[g]
-            return carry
-
-        lax.fori_loop(0, 2, part, 0)
+        for tile in range(3):
+            parts = []
+            for n in range(MODES_DEV):
+                halves = []
+                for half in range(2):
+                    c, sub = divmod(2 * tile + half, 3)
+                    a = first_ref[c, n].astype(F32)[8 * sub : 8 * sub + 8]
+                    b = second_ref[c, n].astype(F32)[8 * sub : 8 * sub + 8]
+                    halves.append(shifted(a, b, sub))
+                parts.append(jnp.concatenate(halves, axis=0).astype(BF))
+            parts = butterfly(parts, lane)
+            for g in range(GROUPS):
+                out_ref[0, g, 16 * tile : 16 * tile + 16, :] = parts[g]
 
     @pl.when(is_low)
     def _():
-        def shifted(a, b, tile):
-            a = pltpu.roll(a, 8 * tile, 1, stride=1, stride_axis=0)
-            b = pltpu.roll(b, 8 * tile, 1, stride=1, stride_axis=0)
-            return jnp.where(lane >= row + 8 * tile, b, a)
+        def shifted(a, b, sub):
+            mixed = jnp.where(lane8 < 128 - 8 * sub - row8, b, a)
+            return pltpu.roll(mixed, 8 * sub, 1, stride=1, stride_axis=0)
 
         run(shifted)
 
     @pl.when(jnp.logical_not(is_low))
     def _():
-        def shifted(a, b, tile):
-            return jnp.where(lane < 127, pltpu.roll(a, 127, 1), pltpu.roll(b, 127, 1))
+        def shifted(a, b, sub):
+            return pltpu.roll(jnp.where(lane8 >= 1, a, b), 127, 1)
 
         run(shifted)
-
-    for g in range(GROUPS):
-        out_ref[0, g] = stage[g].astype(BF)
 
 
 def coeff_blocks(e, coefficients):
@@ -111,7 +110,6 @@
                 pl.BlockSpec(block, lambda k, s: (0, 0, 0, window_high(k, s[0]))),
             ],
             out_specs=pl.BlockSpec((1, GROUPS, 2 * PAIR_DEV, 128), lambda k, s: (k, 0, 0, 0)),
-            scratch_shapes=[pltpu.VMEM((GROUPS, 2 * PAIR_DEV, 128), F32)],
         ),
         compiler_params=pltpu.CompilerParams(vmem_limit_bytes=48 * 2**20),
         name="coeff_blocks",
@@ -130,14 +128,13 @@
         for r in range(32):
             value = shifted(first_ref[r].astype(F32), second_ref[r].astype(F32))
             value = jnp.where(keep, value, 0.0)
-            stage[pl.ds(r, PAIR_DEV, stride=32), :] = value
+            stage[pl.ds(r, PAIR_DEV, stride=ROW_PITCH), :] = value
 
     @pl.when(jnp.logical_and(is_low, k < STEPS))
     def _():
         def shifted(a, b):
-            a = pltpu.roll(a, 0, 1, stride=1, stride_axis=0)
-            b = pltpu.roll(b, 0, 1, stride=1, stride_axis=0)
-            return jnp.where(lane >= row, b, a)
+            mixed = jnp.where(lane < 128 - row, b, a)
+            return pltpu.roll(mixed, 0, 1, stride=1, stride_axis=0)
 
         offset = 128 * k + lane
         run(shifted, (offset >= row) & (offset < L - p0))
@@ -145,7 +142,7 @@
     @pl.when(jnp.logical_and(jnp.logical_not(is_low), k < STEPS))
     def _():
         def shifted(a, b):
-            return jnp.where(lane < 127, pltpu.roll(a, 127, 1), pltpu.roll(b, 127, 1))
+            return pltpu.roll(jnp.where(lane >= 1, a, b), 127, 1)
 
         degree = 128 * high_block + lane
         run(shifted, (degree >= L - 1 - p0 - row) & (degree < L))
@@ -157,7 +154,9 @@
     for q in range(4):
         @pl.when(quarter == q)
         def _():
-            wide[:, 128 * q : 128 * q + 128] = stage[...].astype(BF)
+            for i in range(PAIR_DEV):
+                value = stage[ROW_PITCH * i : ROW_PITCH * i + 32, :].astype(BF)
+                wide[32 * i : 32 * i + 32, 128 * q : 128 * q + 128] = value
 
     @pl.when(quarter == 3)
     def _():
@@ -188,7 +187,7 @@
                 pl.BlockSpec((512, 512), lambda k, s: (0, 0)),
             ],
             out_specs=pl.BlockSpec((PAIR_DEV, 128, 128), lambda k, s: (0, 0, k // 4)),
-            scratch_shapes=[pltpu.VMEM((PAIR_DEV * 32, 128), F32), pltpu.VMEM((PAIR_DEV * 32, 512), BF)],
+            scratch_shapes=[pltpu.VMEM((PAIR_DEV * ROW_PITCH, 128), F32), pltpu.VMEM((PAIR_DEV * 32, 512), BF)],
         ),
         compiler_params=pltpu.CompilerParams(vmem_limit_bytes=48 * 2**20),
         name="angular_blocks",
@@ -200,28 +199,59 @@
     return jnp.where(is_low, p0 // 4 + GROUPS * k, GROUPS * jnp.minimum(high_block, 11))
 
 
-def table_start(k, e):
-    return jnp.minimum(table_first(k, e), L // 4 - GROUPS)
-
-
-def sums_kernel(
-    e_ref, twist_ref, coeff_ref, table_ref, angular_hbm, out_ref, left, right, turned, angular_ref, sem
-):
+def piece_owner(e, other_core, second, first):
+    core = (e + other_core) % 2
+    x, y = (e // 2) % 4, e // 8
+    along_x = jnp.where(core == 0, SHIFTS[first], SHIFTS[second])
+    along_y = jnp.where(core == 0, SHIFTS[second], SHIFTS[first])
+    return (((y + 4 - along_y) % 4) * 4 + (x + 4 - along_x) % 4) * 2 + core
+
+
+def sums_kernel(e_ref, twist_ref, coeff_ref, *refs):
+    gathered, (angular_hbm, out_ref, left, right, turned, table_ref, angular_ref, sems, sem) = refs[:8], refs[8:]
     k = pl.program_id(0)
     e = e_ref[0]
-    _, n_low, _, _ = step_info(k, e)
-    base = table_first(k, e) - table_start(k, e)
+    p0, n_low, _, _ = step_info(k, e)
+    base = table_first(k, e)
     fetch = pltpu.make_async_copy(angular_hbm, angular_ref, sem)
+    first_piece = p0 // 4 // PIECE
 
     @pl.when(k == 0)
     def _():
+        for buffer in range(8):
+            other_core, second = divmod(buffer, 4)
+            for first in range(4):
+                owner = piece_owner(e, other_core, second, first)
+
+                @pl.when(owner >= first_piece)
+                def _():
+                    pltpu.make_async_copy(
+                        gathered[buffer].at[pl.ds(first * PIECE, PIECE)],
+                        table_ref.at[pl.ds(owner * PIECE, PIECE)],
+                        sems.at[owner],
+                    ).start()
+
         fetch.start()
+
+    last_group = L // 4 - 1
+    wait_from = jnp.where(
+        k == 0, first_piece, jnp.minimum(p0 // 4 + GROUPS * k - 1, last_group) // PIECE + 1
+    )
+    wait_to = jnp.minimum(p0 // 4 + GROUPS * k + GROUPS - 1, last_group) // PIECE + 1
+
+    def arrive(piece, carry):
+        pltpu.make_async_copy(
+            gathered[0].at[pl.ds(0, PIECE)], table_ref.at[pl.ds(piece * PIECE, PIECE)], sems.at[piece]
+        ).wait()
+        return carry
+
+    lax.fori_loop(wait_from, wait_to, arrive, 0)
 
     lane = lax.broadcasted_iota(jnp.int32, (64, 128), 1)
     slots = [(lane & 3) == j for j in range(4)]
 
     def group(g, carry):
-        table = table_ref[jnp.minimum(base + g, GROUPS - 1)]
+        table = table_ref[jnp.minimum(base + g, last_group)]
         weights = jnp.concatenate(
             [jnp.where(slots[j], table, jnp.zeros_like(table)) for j in range(4)], axis=0
         )
@@ -291,7 +321,7 @@
         lax.fori_loop(0, 16, pair, 0, unroll=4)
 
 
-def cycle_sums(e, twist, coeffs, table, angular):
+def cycle_sums(e, twist, coeffs, gathered, angular):
     return pl.pallas_call(
         sums_kernel,
         out_shape=jax.ShapeDtypeStruct((8, 32, 16, 96), BF),
@@ -300,24 +330,22 @@
             grid=(STEPS,),
             in_specs=[
                 pl.BlockSpec((1, GROUPS, 48, 128), lambda k, s, t: (k, 0, 0, 0)),
-                pl.BlockSpec(
-                    (pl.Element(GROUPS), pl.Element(64), pl.Element(128)),
-                    lambda k, s, t: (table_start(k, s[0]), 0, 0),
-                ),
-                pl.BlockSpec(memory_space=pl.ANY),
+                *[pl.BlockSpec(memory_space=pl.ANY)] * 9,
             ],
             out_specs=pl.BlockSpec((8, 32, 16, 96), lambda k, s, t: (0, 0, 0, 0)),
             scratch_shapes=[
                 pltpu.VMEM((48 * PITCH, 128), F32),
                 pltpu.VMEM((48 * PITCH, 128), F32),
                 pltpu.VMEM((32 * 96, 128), F32),
+                pltpu.VMEM((L // 4, 64, 128), BF),
                 pltpu.VMEM((PAIR_DEV, 128, KPAD), BF),
+                pltpu.SemaphoreType.DMA((32,)),
                 pltpu.SemaphoreType.DMA,
             ],
         ),
         compiler_params=pltpu.CompilerParams(vmem_limit_bytes=56 * 2**20),
         name="cycle_sums",
-    )(e, twist, coeffs, table, angular)
+    )(e, twist, coeffs, *gathered, angular)
 
 
 SOURCES_STEP = 8
@@ -397,15 +425,70 @@
     )(received, jnp.asarray(pixel_basis()))
 
 
+def table_kernel(r_ref, bessel_ref, counts_ref, out_ref, stage, grouped):
+    width = bessel_ref.shape[3]
+    mode = lax.broadcasted_iota(jnp.int32, (MODES_DEV, width), 0) + MODES_DEV * r_ref[0]
+    live = mode < counts_ref[...]
+    lane = lax.broadcasted_iota(jnp.int32, (8, 128), 1)
+    for owner in range(8):
+        for f in range(2):
+            for shell in range(4):
+                row = (owner * 8 + f * 4 + shell) * ROW_PITCH
+                value = bessel_ref[f, owner * 4 + shell].astype(F32)
+                stage[row : row + MODES_DEV, 0:width] = jnp.where(live, value, 0.0)
+
+    def one(owner, carry):
+        parts = [
+            stage[pl.ds(owner * 8 * ROW_PITCH + n, 8, stride=ROW_PITCH), :] for n in range(MODES_DEV)
+        ]
+        parts = butterfly(parts, lane)
+        for g in range(width // 4):
+            grouped[g, pl.ds(pl.multiple_of(owner * 8, 8), 8), :] = parts[g]
+        return carry
+
+    lax.fori_loop(0, 8, one, 0, unroll=2)
+    for g in range(width // 4):
+        out_ref[g] = grouped[g].astype(BF)
+
+
 def radial_table(bessel, mode_counts):
     width = bessel.shape[3]
     counts = lax.dynamic_slice_in_dim(mode_counts, lax.axis_index("ell") * width, width)
-    modes = lax.axis_index("rad") * MODES_DEV + jnp.arange(MODES_DEV, dtype=jnp.int32)
-    live = modes[:, None] < counts[None, :]
-    table = jnp.where(live, bessel, jnp.zeros_like(bessel))
-    table = table.reshape(2, 8, 4, MODES_DEV, width // 4, 4)
-    table = table.transpose(4, 1, 0, 2, 3, 5)
-    return table.reshape(width // 4, 64, 4 * MODES_DEV)
+    return pl.pallas_call(
+        table_kernel,
+        out_shape=jax.ShapeDtypeStruct((width // 4, 64, 128), BF),
+        grid_spec=pltpu.PrefetchScalarGridSpec(
+            num_scalar_prefetch=1,
+            grid=(1,),
+            in_specs=[
+                pl.BlockSpec(bessel.shape, lambda k, s: (0, 0, 0, 0)),
+                pl.BlockSpec((1, width), lambda k, s: (0, 0)),
+            ],
+            out_specs=pl.BlockSpec((width // 4, 64, 128), lambda k, s: (0, 0, 0)),
+            scratch_shapes=[
+                pltpu.VMEM((64 * ROW_PITCH, 128), F32),
+                pltpu.VMEM((width // 4, 64, 128), F32),
+            ],
+        ),
+        compiler_params=pltpu.CompilerParams(vmem_limit_bytes=32 * 2**20),
+        name="radial_table",
+    )(lax.axis_index("rad").reshape(1).astype(jnp.int32), bessel, counts.reshape(1, width))
+
+
+def ring_shift(value, shift, first):
+    pairs = []
+    for e in range(32):
+        core, x, y = e % 2, (e // 2) % 4, e // 8
+        if (core == 0) == first:
+            x = (x + shift) % 4
+        else:
+            y = (y + shift) % 4
+        pairs.append((e, (y * 4 + x) * 2 + core))
+    return lax.ppermute(value, "ell", pairs)
+
+
+def other_core(value):
+    return lax.ppermute(value, "ell", [(e, e ^ 1) for e in range(32)])
 
 
 def twist_table():
@@ -420,10 +503,18 @@
     e = lax.axis_index("ell")
     e_arr = e.reshape(1).astype(jnp.int32)
     twist = lax.dynamic_index_in_dim(jnp.asarray(twist_table()), e, 0, keepdims=False)
-    table = lax.all_gather(radial_table(bessel, mode_counts), "ell", axis=0, tiled=True)
-    coeffs = coeff_blocks(e_arr, coefficients)
+    table = radial_table(bessel, mode_counts)
+    moved = [ring_shift(table, shift, True) for shift in SHIFTS[1:]]
     angular = angular_blocks(e_arr, legendre)
-    sums = cycle_sums(e_arr, twist, coeffs, table, angular)
+    angular, *moved = lax.optimization_barrier((angular, *moved))
+    own = jnp.concatenate([table, *moved], axis=0)
+    far = [ring_shift(own, shift, False) for shift in SHIFTS[1:]]
+    e_late, own = lax.optimization_barrier((e_arr, own))
+    coeffs = coeff_blocks(e_late, coefficients)
+    coeffs, *far = lax.optimization_barrier((coeffs, *far))
+    mine = [own, *far]
+    gathered = mine + [other_core(value) for value in mine]
+    sums = cycle_sums(e_arr, twist, coeffs, gathered, angular)
     received = lax.all_to_all(
         sums.reshape(256, 16, 96), ("rad", "ell"), split_axis=0, concat_axis=0, tiled=True
     )

time: 149 us -> 127 us (0.85)
  between operations: 14.1 us -> 0.74 us
  starting transfers between devices: 0.04 us -> 12.7 us
  waiting for transfers between devices: 14.6 us -> 2.77 us
  Pallas kernels: 68.5 us -> 61.6 us
  local copies, waits for them, and re-layouts: 9.65 us -> 5.89 us
  blocking collectives: 41.1 us -> 42.8 us
    all_gather x1 -> x0, waiting for transfers between devices: 14.5 us -> none  [local(): lax.all_gather(radial_table(bessel, mode_counts), 'ell', axis=0, tiled=True)]
    ppermute x0 -> x10, starting transfers between devices: none -> 12.7 us  [the longest x6 9.51 us: ring_shift(): return lax.ppermute(value, 'ell', pairs)]
    pallas_call x1, Pallas kernels: 25.9 us -> 18.9 us  [coeff_blocks(): pl.pallas_call(coeff_kernel, out_shape=jax.ShapeDtypeStruct((STEPS, GROUP...]
    ppermute x0 -> x10, waiting for transfers between devices: none -> 2.77 us  [the longest x4 2.76 us: other_core(): return lax.ppermute(value, 'ell', [(e, e ^ 1) for e in range(32)])]
    pallas_call x1, Pallas kernels: 14.3 us -> 11.7 us  [angular_blocks(): pl.pallas_call(angular_kernel, out_shape=jax.ShapeDtypeStruct((PAIR_DEV,...]
    transpose x1 -> x0, local copies, waits for them, and re-layouts: 2.13 us -> none  [radial_table(): table = table.transpose(4, 1, 0, 2, 3, 5)]
    pallas_call x0 -> x1, Pallas kernels: none -> 2.08 us  [radial_table(): pl.pallas_call(table_kernel, out_shape=jax.ShapeDtypeStruct((width // 4,...]
    all_to_all x1, blocking collectives: 41.1 us -> 42.8 us  [local(): lax.all_to_all(sums.reshape(256, 16, 96), ('rad', 'ell'), split_axis=0, c...]
  transfers between devices with their start and end apart: 1 -> 10, of which waited for: 1 -> 3; matrix products, arithmetic and copies ran while one was open for 1% -> 1% of each run, Pallas kernels for 27% -> 24%
where the time goes in v2:
time: 127 us
  Pallas kernels  61.6 us (49%)
  blocking collectives  42.8 us (34%)
  starting transfers between devices  12.7 us (10%)
  local copies, waits for them, and re-layouts  5.89 us (5%)
  waiting for transfers between devices  2.77 us (2%)
    all_to_all x1, blocking collectives, local(): lax.all_to_all(sums.reshape(256, 16, 96), ('rad', 'ell'), split_axis=0, c...  42.8 us
    pallas_call x1, Pallas kernels, cycle_sums(): pl.pallas_call(sums_kernel, out_shape=jax.ShapeDtypeStruct((8, 32, 16, 96...  24 us
    pallas_call x1, Pallas kernels, coeff_blocks(): pl.pallas_call(coeff_kernel, out_shape=jax.ShapeDtypeStruct((STEPS, GROUP...  18.9 us
    pallas_call x1, Pallas kernels, angular_blocks(): pl.pallas_call(angular_kernel, out_shape=jax.ShapeDtypeStruct((PAIR_DEV,...  11.7 us
    ppermute x6, starting transfers between devices, ring_shift(): return lax.ppermute(value, 'ell', pairs)  9.51 us
    pallas_call x1, Pallas kernels, pixels(): pl.pallas_call(pixels_kernel, out_shape=(out, out), grid=(32 // SOURCES_S...  5.02 us
    unnamed x20, local copies, waits for them, and re-layouts  4.52 us
    ppermute x4, starting transfers between devices, other_core(): return lax.ppermute(value, 'ell', [(e, e ^ 1) for e in range(32)])  3.15 us
  transfers between devices with their start and end apart: 10, of which 3 were waited for; matrix products, arithmetic and copies ran while one was open for 1% of the time, Pallas kernels for 24%

profile of v2, /device:TPU:1, one launch (start us, length us, event | category | flops | bytes accessed | tf_op | source)
XLA Modules:
  0.0 126.6 jit_solution(9810589674189603749)
XLA Ops:
  0.6 0.0 copy-start
  0.7 0.7 copy-done
  1.3 0.1 dynamic-slice_bitcast_fusion.1.counts_ref
  1.4 0.0 copy-start.3
  1.4 1.0 copy-done.3
  2.5 0.0 slice-start
  2.5 2.1 %radial_table.1 = bf16[12,64,128]{2,1,0:T(8,128)(2,1)S(1)} custom-call(s32[1]{0:T(128)} %bitcast.2.r_ref, bf16[2,32,32,48]{3,2,1,0:T(8,128)(2,1)S(1)} %copy-done.3, s32[1,48]{1,0:T(1,128)S(1)} %dynamic-slice_bitcast_fusion.1.counts_ref), custom_call_target="tpu_custom_call" | custom-call | tf_op jit(solution)/shard_map/radial_table/pallas_call | solution.py:457
  4.5 3.8 %collective-permute-start.2 = (bf16[12,64,128]{2,1,0:T(8,128)(2,1)S(1)}, bf16[12,64,128]{2,1,0:T(8,128)(2,1)S(1)}, u32[]{:S(2)}, u32[]{:S(2)}) collective-permute-start(bf16[12,64,128]{2,1,0:T(8,128)(2,1)S(1)} %radial_table.1), channel_id=1, source_target_pairs={{0,32},{8,136},{16,48},{24,152},{32,0},{40,168},{48,16},{56,184},{... | collective-permute-start | bytes 589832 | tf_op jit(solution)/shard_map/ppermute | solution.py:487
  8.4 0.8 collective-permute-start.1
  9.1 0.7 collective-permute-start
  9.8 0.0 copy-start.1
  9.8 1.7 %copy-done.1 = bf16[32,24,1537]{2,1,0:T(8,128)(2,1)S(1)} copy-done((bf16[32,24,1537]{2,1,0:T(8,128)(2,1)S(1)}, bf16[32,24,1537]{2,1,0:T(8,128)(2,1)}, u32[]{:S(2)}) %copy-start.1) | copy-done | bytes 2360856
  11.6 0.0 copy-start.2
  11.6 1.0 copy-done.2
  12.6 0.0 slice-start.1
  12.6 11.7 %angular_blocks.1.refs_8_ = bf16[24,128,512]{2,1,0:T(8,128)(2,1)} custom-call(s32[1]{0:T(128)} %bitcast.e_ref, bf16[32,24,1537]{2,1,0:T(8,128)(2,1)S(1)} %copy-done.1, bf16[32,24,1537]{2,1,0:T(8,128)(2,1)S(1)} %copy-done.1, bf16[512,512]{1,0:T(8,128)(2,1)S(1)} %copy-done.2), custom_call_target="tpu_custom_call" | custom-call | tf_op jit(solution)/shard_map/angular_blocks/pallas_call | solution.py:178
  24.3 0.0 collective-permute-done.2
  24.3 0.0 collective-permute-done.1
  24.3 0.0 collective-permute-done
  24.3 0.1 pad_maximum_fusion.refs_0_
  24.4 0.0 copy-start.4
  24.4 2.8 %collective-permute-start.5 = (bf16[48,64,128]{2,1,0:T(8,128)(2,1)S(1)}, bf16[48,64,128]{2,1,0:T(8,128)(2,1)S(1)}, u32[]{:S(2)}, u32[]{:S(2)}) collective-permute-start(bf16[48,64,128]{2,1,0:T(8,128)(2,1)S(1)} %pad_maximum_fusion.refs_0_), channel_id=1, source_target_pairs={{0,128},{8,40},{16,144},{24,56},{32,160},{40,8},{48,176},{56,24},{... | collective-permute-start | bytes 2359304 | tf_op jit(solution)/shard_map/ppermute | solution.py:487
  27.1 0.9 collective-permute-start.4
  28.1 0.5 collective-permute-start.3
  28.6 2.4 %collective-permute-start.6 = (bf16[48,64,128]{2,1,0:T(8,128)(2,1)S(1)}, bf16[48,64,128]{2,1,0:T(8,128)(2,1)}, u32[]{:S(2)}, u32[]{:S(2)}) collective-permute-start(bf16[48,64,128]{2,1,0:T(8,128)(2,1)S(1)} %pad_maximum_fusion.refs_0_), channel_id=1, source_target_pairs={{0,8},{8,0},{16,24},{24,16},{32,40},{40,32},{48,56},{56,48},{64,72... | collective-permute-start | bytes 2359304 | tf_op jit(solution)/shard_map/ppermute | solution.py:491
  31.1 0.0 slice-done
  31.1 0.0 slice-done.1
  31.1 18.9 %coeff_blocks.1.coeff_ref = bf16[14,32,48,128]{3,2,1,0:T(8,128)(2,1)} custom-call(s32[1]{0:T(128)} %bitcast.e_ref, bf16[2,32,24,1537]{3,2,1,0:T(8,128)(2,1)S(1)} %bitcast.9, bf16[2,32,24,1537]{3,2,1,0:T(8,128)(2,1)S(1)} %bitcast.9), custom_call_target="tpu_custom_call" | custom-call | tf_op jit(solution)/shard_map/coeff_blocks/pallas_call | solution.py:102
  49.9 0.0 copy-done.4
  49.9 0.0 collective-permute-done.5.refs_3_
  49.9 0.0 copy-start.5
  50.0 0.0 collective-permute-done.4.refs_2_
  50.0 0.0 copy-start.6
  50.0 0.0 collective-permute-done.3.refs_1_
  50.0 0.0 copy-start.7
  50.0 0.2 collective-permute-start.7
  50.1 0.4 collective-permute-start.8
  50.6 0.1 collective-permute-start.9
  50.7 1.3 %dynamic-slice_bitcast_fusion.twist_ref = f32[3,48]{1,0:T(4,128)} fusion(f32[32,3,48]{2,1,0:T(4,128)} %constant.26.clone, s32[]{:T(128)S(6)} %select_n.7), kind=kLoop, calls=%fused_computation.1 | loop fusion | bytes 1156 | tf_op jit(solution)/shard_map/jit(dynamic_index_in_dim)/squeeze | solution.py:505
  52.0 0.0 collective-permute-done.6.refs_4_
  52.0 0.5 collective-permute-done.7.refs_5_
  52.5 1.1 collective-permute-done.8.refs_6_
  53.6 1.1 collective-permute-done.9.refs_7_
  54.7 0.0 copy-done.5
  54.8 0.0 copy-done.6
  54.8 0.0 copy-done.7
  54.8 24.0 %cycle_sums.1 = bf16[8,32,16,96]{3,2,1,0:T(8,128)(2,1)} custom-call(s32[1]{0:T(128)} %bitcast.e_ref, f32[3,48]{1,0:T(4,128)} %dynamic-slice_bitcast_fusion.twist_ref, bf16[14,32,48,128]{3,2,1,0:T(8,128)(2,1)} %coeff_blocks.1.coeff_ref, bf16[48,64,128]{2,1,0:T(8,128)(2,1)} %copy-done.4, bf16[48,64,128]{2,1,0:T(8,128)(2,1)} %copy-done.7, ...), custom_call_target="tpu_custom_call" | custom-call | tf_op jit(solution)/shard_map/cycle_sums/pallas_call | solution.py:325
  78.8 42.8 %all_to_all.5 = bf16[256,16,96]{2,1,0:T(8,128)(2,1)S(1)} all-to-all(bf16[256,16,96]{2,1,0:T(8,128)(2,1)} %bitcast.11), channel_id=1, replica_groups=mesh['ell'=32,'rad'=8] {'rad','ell'}, dimensions={0} | all-to-all | bytes 1572864 | tf_op jit(solution)/shard_map/all_to_all | solution.py:518
  121.6 5.0 %pixels.1 = (f32[4,2,2048]{2,1,0:T(2,128)}, f32[4,2,2048]{2,1,0:T(2,128)}) custom-call(bf16[8,32,16,96]{3,2,1,0:T(8,128)(2,1)S(1)} %bitcast.10, bf16[32,96,1024]{2,1,0:T(8,128)(2,1)} %constant.28.clone.basis_ref), custom_call_target="tpu_custom_call" | custom-call | tf_op jit(solution)/shard_map/pixels/pallas_call | solution.py:413
  (1 shorter events, 0.0 us)
Async XLA Ops:
  0.6 0.7 copy-start
  1.4 1.0 copy-start.3
  2.5 28.6 %slice-start = ((s8[5111808]{0:T(1024)(128)(4,1)}), s8[4194304]{0:T(1024)(128)(4,1)S(1)}, s32[]{:S(2)}) async-start(s8[5111808]{0:T(1024)(128)(4,1)} %bitcast.8), calls=%async_computation.1 | async-start | bytes 8388608
  4.5 19.7 %collective-permute-start.2 = (bf16[12,64,128]{2,1,0:T(8,128)(2,1)S(1)}, bf16[12,64,128]{2,1,0:T(8,128)(2,1)S(1)}, u32[]{:S(2)}, u32[]{:S(2)}) collective-permute-start(bf16[12,64,128]{2,1,0:T(8,128)(2,1)S(1)} %radial_table.1), channel_id=1, source_target_pairs={{0,32},{8,136},{16,48},{24,152},{32,0},{40,168},{48,16},{56,184},{... | collective-permute-start | bytes 589832 | tf_op jit(solution)/shard_map/ppermute | solution.py:487
  8.4 15.9 %collective-permute-start.1 = (bf16[12,64,128]{2,1,0:T(8,128)(2,1)S(1)}, bf16[12,64,128]{2,1,0:T(8,128)(2,1)S(1)}, u32[]{:S(2)}, u32[]{:S(2)}) collective-permute-start(bf16[12,64,128]{2,1,0:T(8,128)(2,1)S(1)} %radial_table.1), channel_id=1, source_target_pairs={{0,48},{8,200},{16,0},{24,216},{32,16},{40,232},{48,32},{56,248},{... | collective-permute-start | bytes 589832 | tf_op jit(solution)/shard_map/ppermute | solution.py:487
  9.1 15.1 %collective-permute-start = (bf16[12,64,128]{2,1,0:T(8,128)(2,1)S(1)}, bf16[12,64,128]{2,1,0:T(8,128)(2,1)S(1)}, u32[]{:S(2)}, u32[]{:S(2)}) collective-permute-start(bf16[12,64,128]{2,1,0:T(8,128)(2,1)S(1)} %radial_table.1), channel_id=1, source_target_pairs={{0,16},{8,72},{16,32},{24,88},{32,48},{40,104},{48,0},{56,120},{64... | collective-permute-start | bytes 589832 | tf_op jit(solution)/shard_map/ppermute | solution.py:487
  9.8 1.7 %copy-start.1 = (bf16[32,24,1537]{2,1,0:T(8,128)(2,1)S(1)}, bf16[32,24,1537]{2,1,0:T(8,128)(2,1)}, u32[]{:S(2)}) copy-start(bf16[32,24,1537]{2,1,0:T(8,128)(2,1)} %second_ref.2) | copy-start | bytes 7082500
  11.6 1.0 copy-start.2
  12.6 18.5 %slice-start.1 = ((s8[5111808]{0:T(1024)(128)(4,1)}), s8[917504]{0:T(1024)(128)(4,1)S(1)}, s32[]{:S(2)}) async-start(s8[5111808]{0:T(1024)(128)(4,1)} %bitcast.8), calls=%async_computation.2 | async-start | bytes 1835008
  24.4 25.6 %copy-start.4 = (bf16[48,64,128]{2,1,0:T(8,128)(2,1)}, bf16[48,64,128]{2,1,0:T(8,128)(2,1)S(1)}, u32[]{:S(2)}) copy-start(bf16[48,64,128]{2,1,0:T(8,128)(2,1)S(1)} %pad_maximum_fusion.refs_0_) | copy-start | bytes 2359300
  24.4 25.6 %collective-permute-start.5 = (bf16[48,64,128]{2,1,0:T(8,128)(2,1)S(1)}, bf16[48,64,128]{2,1,0:T(8,128)(2,1)S(1)}, u32[]{:S(2)}, u32[]{:S(2)}) collective-permute-start(bf16[48,64,128]{2,1,0:T(8,128)(2,1)S(1)} %pad_maximum_fusion.refs_0_), channel_id=1, source_target_pairs={{0,128},{8,40},{16,144},{24,56},{32,160},{40,8},{48,176},{56,24},{... | collective-permute-start | bytes 2359304 | tf_op jit(solution)/shard_map/ppermute | solution.py:487
  27.1 22.8 %collective-permute-start.4 = (bf16[48,64,128]{2,1,0:T(8,128)(2,1)S(1)}, bf16[48,64,128]{2,1,0:T(8,128)(2,1)S(1)}, u32[]{:S(2)}, u32[]{:S(2)}) collective-permute-start(bf16[48,64,128]{2,1,0:T(8,128)(2,1)S(1)} %pad_maximum_fusion.refs_0_), channel_id=1, source_target_pairs={{0,192},{8,56},{16,208},{24,8},{32,224},{40,24},{48,240},{56,40},{... | collective-permute-start | bytes 2359304 | tf_op jit(solution)/shard_map/ppermute | solution.py:487
  28.1 21.9 %collective-permute-start.3 = (bf16[48,64,128]{2,1,0:T(8,128)(2,1)S(1)}, bf16[48,64,128]{2,1,0:T(8,128)(2,1)S(1)}, u32[]{:S(2)}, u32[]{:S(2)}) collective-permute-start(bf16[48,64,128]{2,1,0:T(8,128)(2,1)S(1)} %pad_maximum_fusion.refs_0_), channel_id=1, source_target_pairs={{0,64},{8,24},{16,80},{24,40},{32,96},{40,56},{48,112},{56,8},{64,... | collective-permute-start | bytes 2359304 | tf_op jit(solution)/shard_map/ppermute | solution.py:487
  28.6 23.4 %collective-permute-start.6 = (bf16[48,64,128]{2,1,0:T(8,128)(2,1)S(1)}, bf16[48,64,128]{2,1,0:T(8,128)(2,1)}, u32[]{:S(2)}, u32[]{:S(2)}) collective-permute-start(bf16[48,64,128]{2,1,0:T(8,128)(2,1)S(1)} %pad_maximum_fusion.refs_0_), channel_id=1, source_target_pairs={{0,8},{8,0},{16,24},{24,16},{32,40},{40,32},{48,56},{56,48},{64,72... | collective-permute-start | bytes 2359304 | tf_op jit(solution)/shard_map/ppermute | solution.py:491
  49.9 4.8 %copy-start.5 = (bf16[48,64,128]{2,1,0:T(8,128)(2,1)}, bf16[48,64,128]{2,1,0:T(8,128)(2,1)S(1)}, u32[]{:S(2)}) copy-start(bf16[48,64,128]{2,1,0:T(8,128)(2,1)S(1)} %collective-permute-done.5.refs_3_) | copy-start | bytes 2359300
  50.0 4.8 %copy-start.6 = (bf16[48,64,128]{2,1,0:T(8,128)(2,1)}, bf16[48,64,128]{2,1,0:T(8,128)(2,1)S(1)}, u32[]{:S(2)}) copy-start(bf16[48,64,128]{2,1,0:T(8,128)(2,1)S(1)} %collective-permute-done.4.refs_2_) | copy-start | bytes 2359300
  50.0 4.8 %copy-start.7 = (bf16[48,64,128]{2,1,0:T(8,128)(2,1)}, bf16[48,64,128]{2,1,0:T(8,128)(2,1)S(1)}, u32[]{:S(2)}) copy-start(bf16[48,64,128]{2,1,0:T(8,128)(2,1)S(1)} %collective-permute-done.3.refs_1_) | copy-start | bytes 2359300
  50.0 2.5 %collective-permute-start.7 = (bf16[48,64,128]{2,1,0:T(8,128)(2,1)S(1)}, bf16[48,64,128]{2,1,0:T(8,128)(2,1)}, u32[]{:S(2)}, u32[]{:S(2)}) collective-permute-start(bf16[48,64,128]{2,1,0:T(8,128)(2,1)S(1)} %collective-permute-done.3.refs_1_), channel_id=1, source_target_pairs={{0,8},{8,0},{16,24},{24,16},{32,40},{40,32},{48,56},{56,48},{64,72... | collective-permute-start | bytes 2359304 | tf_op jit(solution)/shard_map/ppermute | solution.py:491
  50.1 3.5 %collective-permute-start.8 = (bf16[48,64,128]{2,1,0:T(8,128)(2,1)S(1)}, bf16[48,64,128]{2,1,0:T(8,128)(2,1)}, u32[]{:S(2)}, u32[]{:S(2)}) collective-permute-start(bf16[48,64,128]{2,1,0:T(8,128)(2,1)S(1)} %collective-permute-done.4.refs_2_), channel_id=1, source_target_pairs={{0,8},{8,0},{16,24},{24,16},{32,40},{40,32},{48,56},{56,48},{64,72... | collective-permute-start | bytes 2359304 | tf_op jit(solution)/shard_map/ppermute | solution.py:491
  50.6 4.2 %collective-permute-start.9 = (bf16[48,64,128]{2,1,0:T(8,128)(2,1)S(1)}, bf16[48,64,128]{2,1,0:T(8,128)(2,1)}, u32[]{:S(2)}, u32[]{:S(2)}) collective-permute-start(bf16[48,64,128]{2,1,0:T(8,128)(2,1)S(1)} %collective-permute-done.5.refs_3_), channel_id=1, source_target_pairs={{0,8},{8,0},{16,24},{24,16},{32,40},{40,32},{48,56},{56,48},{64,72... | collective-permute-start | bytes 2359304 | tf_op jit(solution)/shard_map/ppermute | solution.py:491

commit v3 on v2

--- a/solution.py
+++ b/solution.py
@@ -54,6 +54,11 @@
                 continue
             high = low | (1 << bit)
             first, second = parts[low], parts[high]
+            if distance == 64:
+                swapped = pltpu.roll(jnp.where(upper, first, second), 64, 1)
+                parts[low] = jnp.where(upper, swapped, first)
+                parts[high] = jnp.where(upper, second, swapped)
+                continue
             parts[low] = jnp.where(upper, pltpu.roll(second, distance, 1), first)
             parts[high] = jnp.where(upper, second, pltpu.roll(first, 128 - distance, 1))
     return parts
@@ -116,11 +121,21 @@
     )(e, coefficients, coefficients)
 
 
-def angular_kernel(e_ref, first_ref, second_ref, pick_ref, out_ref, stage, wide):
+def angular_kernel(e_ref, first_ref, second_ref, out_ref, stage, wide, pick_ref):
     k = pl.program_id(0)
     e = e_ref[0]
     p0, _, is_low, high_block = step_info(k, e)
     quarter = k % 4
+
+    @pl.when(k == 0)
+    def _():
+        slot = lax.broadcasted_iota(jnp.int32, (512, 128), 0)
+        column = lax.broadcasted_iota(jnp.int32, (512, 128), 1)
+        group = 32 * (slot >> 7) + ((slot & 127) >> 2)
+        for j in range(4):
+            hit = (column == group) & ((slot & 3) == j)
+            pick_ref[:, 128 * j : 128 * j + 128] = jnp.where(hit, 1.0, 0.0).astype(BF)
+
     lane = lax.broadcasted_iota(jnp.int32, (PAIR_DEV, 128), 1)
     row = lax.broadcasted_iota(jnp.int32, (PAIR_DEV, 128), 0)
 
@@ -170,11 +185,6 @@
 
 def angular_blocks(e, legendre):
     block = (32, PAIR_DEV, 128)
-    pick = np.zeros((512, 512), np.float32)
-    for q in range(4):
-        for g in range(32):
-            for j in range(4):
-                pick[128 * q + 4 * g + j, 128 * j + 32 * q + g] = 1.0
     return pl.pallas_call(
         angular_kernel,
         out_shape=jax.ShapeDtypeStruct((PAIR_DEV, 128, KPAD), BF),
@@ -184,14 +194,13 @@
             in_specs=[
                 pl.BlockSpec(block, lambda k, s: (0, 0, window_low(jnp.minimum(k, STEPS - 1), s[0]))),
                 pl.BlockSpec(block, lambda k, s: (0, 0, window_high(jnp.minimum(k, STEPS - 1), s[0]))),
-                pl.BlockSpec((512, 512), lambda k, s: (0, 0)),
             ],
             out_specs=pl.BlockSpec((PAIR_DEV, 128, 128), lambda k, s: (0, 0, k // 4)),
-            scratch_shapes=[pltpu.VMEM((PAIR_DEV * ROW_PITCH, 128), F32), pltpu.VMEM((PAIR_DEV * 32, 512), BF)],
+            scratch_shapes=[pltpu.VMEM((PAIR_DEV * ROW_PITCH, 128), F32), pltpu.VMEM((PAIR_DEV * 32, 512), BF), pltpu.VMEM((512, 512), BF)],
         ),
         compiler_params=pltpu.CompilerParams(vmem_limit_bytes=48 * 2**20),
         name="angular_blocks",
-    )(e, legendre, legendre, jnp.asarray(pick, BF))
+    )(e, legendre, legendre)
 
 
 def table_first(k, e):
@@ -296,9 +305,9 @@
                     sign = jnp.where((i + seg) % 2 == 0, 1.0, -1.0)
                     folded[c][seg] = jnp.where(near, total + other, (other - total) * sign)
             for seg in range(2):
-                scale = twist_ref[2, seg * PAIR_DEV + i]
-                cos = jnp.where(even_row, twist_ref[0, seg * PAIR_DEV + i], scale)
-                sin = jnp.where(even_row, twist_ref[1, seg * PAIR_DEV + i], 0.0)
+                scale = twist_ref[3 * e + 2, seg * PAIR_DEV + i]
+                cos = jnp.where(even_row, twist_ref[3 * e, seg * PAIR_DEV + i], scale)
+                sin = jnp.where(even_row, twist_ref[3 * e + 1, seg * PAIR_DEV + i], 0.0)
                 real, imag = folded[0][seg], folded[1][seg]
                 turned[pl.ds(seg * 48 + i, 32, stride=96), :] = real * cos + imag * sin
                 turned[pl.ds(seg * 48 + PAIR_DEV + i, 32, stride=96), :] = imag * cos - real * sin
@@ -311,11 +320,14 @@
                 jnp.transpose(turned[pl.ds(pl.multiple_of((2 * q + d) * 96, 8), 96), :])
                 for d in range(2)
             ]
-            for owner in range(8):
-                north = [x[8 * owner : 8 * owner + 8] for x in rows]
-                south = [x[64 + 8 * owner : 72 + 8 * owner] for x in rows]
-                out_ref[owner, q] = jnp.concatenate(north, axis=0).astype(BF)
-                out_ref[owner, 31 - q] = jnp.concatenate(south[::-1], axis=0).astype(BF)
+            for side, order in ((0, rows), (1, rows[::-1])):
+                packed = jnp.concatenate(
+                    [x[64 * side + 32 * f : 64 * side + 32 * f + 32] for x in order for f in range(2)],
+                    axis=1,
+                )
+                for owner in range(8):
+                    value = packed[4 * owner : 4 * owner + 4].astype(BF)
+                    out_ref[owner, 31 - q if side else q] = value
             return carry
 
         lax.fori_loop(0, 16, pair, 0, unroll=4)
@@ -324,7 +336,7 @@
 def cycle_sums(e, twist, coeffs, gathered, angular):
     return pl.pallas_call(
         sums_kernel,
-        out_shape=jax.ShapeDtypeStruct((8, 32, 16, 96), BF),
+        out_shape=jax.ShapeDtypeStruct((8, 32, 4, 384), BF),
         grid_spec=pltpu.PrefetchScalarGridSpec(
             num_scalar_prefetch=2,
             grid=(STEPS,),
@@ -332,7 +344,7 @@
                 pl.BlockSpec((1, GROUPS, 48, 128), lambda k, s, t: (k, 0, 0, 0)),
                 *[pl.BlockSpec(memory_space=pl.ANY)] * 9,
             ],
-            out_specs=pl.BlockSpec((8, 32, 16, 96), lambda k, s, t: (0, 0, 0, 0)),
+            out_specs=pl.BlockSpec((8, 32, 4, 384), lambda k, s, t: (0, 0, 0, 0)),
             scratch_shapes=[
                 pltpu.VMEM((48 * PITCH, 128), F32),
                 pltpu.VMEM((48 * PITCH, 128), F32),
@@ -361,6 +373,7 @@
         value = in_ref[0, source].astype(F32)
         for radial in range(1, 8):
             value = value + in_ref[radial, source].astype(F32)
+        value = jnp.concatenate([value[:, 96 * part : 96 * part + 96] for part in range(4)], axis=0)
         top = value.astype(BF).astype(F32)
         rest = value - top
         rows = jnp.concatenate(
@@ -415,7 +428,7 @@
         out_shape=(out, out),
         grid=(32 // SOURCES_STEP,),
         in_specs=[
-            pl.BlockSpec((8, SOURCES_STEP, 16, 96), lambda k: (0, k, 0, 0)),
+            pl.BlockSpec((8, SOURCES_STEP, 4, 384), lambda k: (0, k, 0, 0)),
             pl.BlockSpec((SOURCES_STEP, 96, HALF_PIX), lambda k: (k, 0, 0)),
         ],
         out_specs=(spec, spec),
@@ -433,7 +446,7 @@
     for owner in range(8):
         for f in range(2):
             for shell in range(4):
-                row = (owner * 8 + f * 4 + shell) * ROW_PITCH
+                row = (f * 32 + owner * 4 + shell) * ROW_PITCH
                 value = bessel_ref[f, owner * 4 + shell].astype(F32)
                 stage[row : row + MODES_DEV, 0:width] = jnp.where(live, value, 0.0)
 
@@ -496,13 +509,13 @@
     orders = np.concatenate([low, L - 1 - low], axis=1)
     weight = np.where(orders == 0, 1.0, 2.0)
     angle = 2.0 * math.pi / 4096 * orders
-    return np.stack([weight * np.cos(angle), weight * np.sin(angle), weight], axis=1).astype(np.float32)
+    return np.stack([weight * np.cos(angle), weight * np.sin(angle), weight], axis=1).reshape(96, 48).astype(np.float32)
 
 
 def local(coefficients, legendre, bessel, mode_counts):
     e = lax.axis_index("ell")
     e_arr = e.reshape(1).astype(jnp.int32)
-    twist = lax.dynamic_index_in_dim(jnp.asarray(twist_table()), e, 0, keepdims=False)
+    twist = jnp.asarray(twist_table())
     table = radial_table(bessel, mode_counts)
     moved = [ring_shift(table, shift, True) for shift in SHIFTS[1:]]
     angular = angular_blocks(e_arr, legendre)
@@ -516,9 +529,9 @@
     gathered = mine + [other_core(value) for value in mine]
     sums = cycle_sums(e_arr, twist, coeffs, gathered, angular)
     received = lax.all_to_all(
-        sums.reshape(256, 16, 96), ("rad", "ell"), split_axis=0, concat_axis=0, tiled=True
+        sums.reshape(256, 4, 384), ("rad", "ell"), split_axis=0, concat_axis=0, tiled=True
     )
-    return pixels(received.reshape(8, 32, 16, 96))
+    return pixels(received.reshape(8, 32, 4, 384))
 
 
 def solution(mesh):

time: 127 us -> 121 us (0.953)
  blocking collectives: 42.8 us -> 37.7 us
  local copies, waits for them, and re-layouts: 5.89 us -> 4.46 us
    all_to_all x1, blocking collectives: 42.8 us -> 37.7 us  [local(): lax.all_to_all(sums.reshape(256, 4, 384), ('rad', 'ell'), split_axis=0, c...]
    pallas_call x1, Pallas kernels: 11.7 us -> 9.8 us  [angular_blocks(): pl.pallas_call(angular_kernel, out_shape=jax.ShapeDtypeStruct((PAIR_DEV,...]
    pallas_call x1, Pallas kernels: 24 us -> 25.4 us  [cycle_sums(): pl.pallas_call(sums_kernel, out_shape=jax.ShapeDtypeStruct((8, 32, 4, 384...]
    squeeze x1 -> x0, local copies, waits for them, and re-layouts: 1.29 us -> none  [local(): lax.dynamic_index_in_dim(jnp.asarray(twist_table()), e, 0, keepdims=False)]
    unnamed x20 -> x28, local copies, waits for them, and re-layouts: 4.52 us -> 4.38 us
  transfers between devices with their start and end apart: 10 -> 10, of which waited for: 3 -> 3; matrix products, arithmetic and copies ran while one was open for 1% -> 0% of each run, Pallas kernels for 24% -> 23%
where the time goes in v3:
time: 121 us
  Pallas kernels  61 us (50%)
  blocking collectives  37.7 us (31%)
  starting transfers between devices  12.6 us (10%)
  local copies, waits for them, and re-layouts  4.46 us (4%)
  waiting for transfers between devices  3.93 us (3%)
    all_to_all x1, blocking collectives, local(): lax.all_to_all(sums.reshape(256, 4, 384), ('rad', 'ell'), split_axis=0, c...  37.7 us
    pallas_call x1, Pallas kernels, cycle_sums(): pl.pallas_call(sums_kernel, out_shape=jax.ShapeDtypeStruct((8, 32, 4, 384...  25.4 us
    pallas_call x1, Pallas kernels, coeff_blocks(): pl.pallas_call(coeff_kernel, out_shape=jax.ShapeDtypeStruct((STEPS, GROUP...  18.5 us
    pallas_call x1, Pallas kernels, angular_blocks(): pl.pallas_call(angular_kernel, out_shape=jax.ShapeDtypeStruct((PAIR_DEV,...  9.8 us
    ppermute x6, starting transfers between devices, ring_shift(): return lax.ppermute(value, 'ell', pairs)  9.58 us
    pallas_call x1, Pallas kernels, pixels(): pl.pallas_call(pixels_kernel, out_shape=(out, out), grid=(32 // SOURCES_S...  5.25 us
    unnamed x28, local copies, waits for them, and re-layouts  4.38 us
    ppermute x4, waiting for transfers between devices, other_core(): return lax.ppermute(value, 'ell', [(e, e ^ 1) for e in range(32)])  3.92 us
  transfers between devices with their start and end apart: 10, of which 3 were waited for; matrix products, arithmetic and copies ran while one was open for 0% of the time, Pallas kernels for 23%

profile of v3, /device:TPU:1, one launch (start us, length us, event | category | flops | bytes accessed | tf_op | source)
XLA Modules:
  0.0 120.7 jit_solution(12666477226398354081)
XLA Ops:
  0.6 0.0 copy-start
  0.7 0.7 copy-done
  1.3 0.1 dynamic-slice_bitcast_fusion.counts_ref
  1.4 0.0 copy-start.3
  1.4 1.0 copy-done.3
  2.5 0.0 slice-start
  2.5 2.1 %radial_table.1 = bf16[12,64,128]{2,1,0:T(8,128)(2,1)S(1)} custom-call(s32[1]{0:T(128)} %bitcast.1.r_ref, bf16[2,32,32,48]{3,2,1,0:T(8,128)(2,1)S(1)} %copy-done.3, s32[1,48]{1,0:T(1,128)S(1)} %dynamic-slice_bitcast_fusion.counts_ref), custom_call_target="tpu_custom_call" | custom-call | tf_op jit(solution)/shard_map/radial_table/pallas_call | solution.py:470
  4.6 3.8 %collective-permute-start.2 = (bf16[12,64,128]{2,1,0:T(8,128)(2,1)S(1)}, bf16[12,64,128]{2,1,0:T(8,128)(2,1)S(1)}, u32[]{:S(2)}, u32[]{:S(2)}) collective-permute-start(bf16[12,64,128]{2,1,0:T(8,128)(2,1)S(1)} %radial_table.1), channel_id=1, source_target_pairs={{0,32},{8,136},{16,48},{24,152},{32,0},{40,168},{48,16},{56,184},{... | collective-permute-start | bytes 589832 | tf_op jit(solution)/shard_map/ppermute | solution.py:500
  8.4 0.8 collective-permute-start.1
  9.2 0.7 collective-permute-start
  9.9 0.0 copy-start.2
  9.9 1.7 %copy-done.2 = bf16[32,24,1537]{2,1,0:T(8,128)(2,1)S(1)} copy-done((bf16[32,24,1537]{2,1,0:T(8,128)(2,1)S(1)}, bf16[32,24,1537]{2,1,0:T(8,128)(2,1)}, u32[]{:S(2)}) %copy-start.2) | copy-done | bytes 2360856
  11.6 0.0 slice-start.1
  11.6 9.8 %angular_blocks.1.refs_8_ = bf16[24,128,512]{2,1,0:T(8,128)(2,1)S(1)} custom-call(s32[1]{0:T(128)} %bitcast.e_ref, bf16[32,24,1537]{2,1,0:T(8,128)(2,1)S(1)} %copy-done.2, bf16[32,24,1537]{2,1,0:T(8,128)(2,1)S(1)} %copy-done.2), custom_call_target="tpu_custom_call" | custom-call | tf_op jit(solution)/shard_map/angular_blocks/pallas_call | solution.py:188
  21.4 0.0 copy-start.1
  21.4 0.0 collective-permute-done.2
  21.4 0.0 collective-permute-done.1
  21.5 0.0 collective-permute-done
  21.5 0.1 pad_maximum_fusion.refs_0_
  21.6 0.0 copy-start.4
  21.6 2.8 %collective-permute-start.5 = (bf16[48,64,128]{2,1,0:T(8,128)(2,1)S(1)}, bf16[48,64,128]{2,1,0:T(8,128)(2,1)S(1)}, u32[]{:S(2)}, u32[]{:S(2)}) collective-permute-start(bf16[48,64,128]{2,1,0:T(8,128)(2,1)S(1)} %pad_maximum_fusion.refs_0_), channel_id=1, source_target_pairs={{0,128},{8,40},{16,144},{24,56},{32,160},{40,8},{48,176},{56,24},{... | collective-permute-start | bytes 2359304 | tf_op jit(solution)/shard_map/ppermute | solution.py:500
  24.4 0.9 collective-permute-start.4
  25.3 0.6 collective-permute-start.3
  25.9 2.3 %collective-permute-start.6 = (bf16[48,64,128]{2,1,0:T(8,128)(2,1)S(1)}, bf16[48,64,128]{2,1,0:T(8,128)(2,1)S(1)}, u32[]{:S(2)}, u32[]{:S(2)}) collective-permute-start(bf16[48,64,128]{2,1,0:T(8,128)(2,1)S(1)} %pad_maximum_fusion.refs_0_), channel_id=1, source_target_pairs={{0,8},{8,0},{16,24},{24,16},{32,40},{40,32},{48,56},{56,48},{64,72... | collective-permute-start | bytes 2359304 | tf_op jit(solution)/shard_map/ppermute | solution.py:504
  28.2 0.0 slice-done
  28.2 0.0 slice-done.1
  28.2 18.5 %coeff_blocks.1.coeff_ref = bf16[14,32,48,128]{3,2,1,0:T(8,128)(2,1)} custom-call(s32[1]{0:T(128)} %bitcast.e_ref, bf16[2,32,24,1537]{3,2,1,0:T(8,128)(2,1)S(1)} %bitcast.7, bf16[2,32,24,1537]{3,2,1,0:T(8,128)(2,1)S(1)} %bitcast.7), custom_call_target="tpu_custom_call" | custom-call | tf_op jit(solution)/shard_map/coeff_blocks/pallas_call | solution.py:107
  46.7 0.0 copy-done.1
  46.7 0.0 copy-done.4
  46.7 0.0 collective-permute-done.5.refs_3_
  46.7 0.0 copy-start.5
  46.7 0.0 collective-permute-done.4.refs_2_
  46.7 0.0 copy-start.6
  46.7 0.0 collective-permute-done.3.refs_1_
  46.8 0.0 copy-start.7
  46.8 0.2 collective-permute-start.7
  46.9 0.4 collective-permute-start.8
  47.4 0.1 collective-permute-start.9
  47.5 0.0 collective-permute-done.6.refs_4_
  47.5 0.0 copy-start.8
  47.5 1.7 %collective-permute-done.7.refs_5_ = bf16[48,64,128]{2,1,0:T(8,128)(2,1)S(1)} collective-permute-done((bf16[48,64,128]{2,1,0:T(8,128)(2,1)S(1)}, bf16[48,64,128]{2,1,0:T(8,128)(2,1)S(1)}, u32[]{:S(2)}, u32[]{:S(2)}) %collective-permute-start.7) | collective-permute-done | bytes 786464 | tf_op jit(solution)/shard_map/ppermute | solution.py:504
  49.1 0.0 copy-start.9
  49.1 1.1 collective-permute-done.8.refs_6_
  50.3 0.0 copy-start.10
  50.3 1.1 collective-permute-done.9.refs_7_
  51.4 0.0 copy-done.5
  51.4 0.0 copy-done.6
  51.4 0.0 copy-done.7
  51.4 0.0 copy-done.8
  51.4 0.0 copy-done.9
  51.4 0.0 copy-done.10
  51.4 0.0 copy-start.11
  51.4 0.9 copy-done.11
  52.3 25.4 %cycle_sums.1 = bf16[8,32,4,384]{3,2,1,0:T(4,128)(2,1)} custom-call(s32[1]{0:T(128)} %bitcast.e_ref, f32[96,48]{1,0:T(8,128)} %constant.19.clone.twist_ref, bf16[14,32,48,128]{3,2,1,0:T(8,128)(2,1)} %coeff_blocks.1.coeff_ref, bf16[48,64,128]{2,1,0:T(8,128)(2,1)} %copy-done.4, bf16[48,64,128]{2,1,0:T(8,128)(2,1)} %copy-done.7, ...), custom_call_target="tpu_custom_call" | custom-call | tf_op jit(solution)/shard_map/cycle_sums/pallas_call | solution.py:337
  77.7 37.7 %all_to_all.5 = bf16[256,4,384]{2,1,0:T(4,128)(2,1)S(1)} all-to-all(bf16[256,4,384]{2,1,0:T(4,128)(2,1)} %bitcast.9), channel_id=1, replica_groups=mesh['ell'=32,'rad'=8] {'rad','ell'}, dimensions={0} | all-to-all | bytes 1572864 | tf_op jit(solution)/shard_map/all_to_all | solution.py:531
  115.5 5.2 %pixels.1 = (f32[4,2,2048]{2,1,0:T(2,128)}, f32[4,2,2048]{2,1,0:T(2,128)}) custom-call(bf16[8,32,4,384]{3,2,1,0:T(4,128)(2,1)S(1)} %bitcast.8, bf16[32,96,1024]{2,1,0:T(8,128)(2,1)} %constant.20.clone.basis_ref), custom_call_target="tpu_custom_call" | custom-call | tf_op jit(solution)/shard_map/pixels/pallas_call | solution.py:426
  (1 shorter events, 0.0 us)
Async XLA Ops:
  0.6 0.7 copy-start
  1.4 1.0 copy-start.3
  2.5 25.8 %slice-start = ((s8[5111808]{0:T(1024)(128)(4,1)}), s8[4194304]{0:T(1024)(128)(4,1)S(1)}, s32[]{:S(2)}) async-start(s8[5111808]{0:T(1024)(128)(4,1)} %bitcast.6), calls=%async_computation.1 | async-start | bytes 8388608
  4.6 16.8 %collective-permute-start.2 = (bf16[12,64,128]{2,1,0:T(8,128)(2,1)S(1)}, bf16[12,64,128]{2,1,0:T(8,128)(2,1)S(1)}, u32[]{:S(2)}, u32[]{:S(2)}) collective-permute-start(bf16[12,64,128]{2,1,0:T(8,128)(2,1)S(1)} %radial_table.1), channel_id=1, source_target_pairs={{0,32},{8,136},{16,48},{24,152},{32,0},{40,168},{48,16},{56,184},{... | collective-permute-start | bytes 589832 | tf_op jit(solution)/shard_map/ppermute | solution.py:500
  8.4 13.0 %collective-permute-start.1 = (bf16[12,64,128]{2,1,0:T(8,128)(2,1)S(1)}, bf16[12,64,128]{2,1,0:T(8,128)(2,1)S(1)}, u32[]{:S(2)}, u32[]{:S(2)}) collective-permute-start(bf16[12,64,128]{2,1,0:T(8,128)(2,1)S(1)} %radial_table.1), channel_id=1, source_target_pairs={{0,48},{8,200},{16,0},{24,216},{32,16},{40,232},{48,32},{56,248},{... | collective-permute-start | bytes 589832 | tf_op jit(solution)/shard_map/ppermute | solution.py:500
  9.2 12.3 %collective-permute-start = (bf16[12,64,128]{2,1,0:T(8,128)(2,1)S(1)}, bf16[12,64,128]{2,1,0:T(8,128)(2,1)S(1)}, u32[]{:S(2)}, u32[]{:S(2)}) collective-permute-start(bf16[12,64,128]{2,1,0:T(8,128)(2,1)S(1)} %radial_table.1), channel_id=1, source_target_pairs={{0,16},{8,72},{16,32},{24,88},{32,48},{40,104},{48,0},{56,120},{64... | collective-permute-start | bytes 589832 | tf_op jit(solution)/shard_map/ppermute | solution.py:500
  9.9 1.7 %copy-start.2 = (bf16[32,24,1537]{2,1,0:T(8,128)(2,1)S(1)}, bf16[32,24,1537]{2,1,0:T(8,128)(2,1)}, u32[]{:S(2)}) copy-start(bf16[32,24,1537]{2,1,0:T(8,128)(2,1)} %second_ref.2) | copy-start | bytes 7082500
  11.6 16.6 %slice-start.1 = ((s8[5111808]{0:T(1024)(128)(4,1)}), s8[917504]{0:T(1024)(128)(4,1)S(1)}, s32[]{:S(2)}) async-start(s8[5111808]{0:T(1024)(128)(4,1)} %bitcast.6), calls=%async_computation.2 | async-start | bytes 1835008
  21.4 25.3 %copy-start.1 = (bf16[24,128,512]{2,1,0:T(8,128)(2,1)}, bf16[24,128,512]{2,1,0:T(8,128)(2,1)S(1)}, u32[]{:S(2)}) copy-start(bf16[24,128,512]{2,1,0:T(8,128)(2,1)S(1)} %angular_blocks.1.refs_8_) | copy-start | bytes 9437188
  21.6 25.1 %copy-start.4 = (bf16[48,64,128]{2,1,0:T(8,128)(2,1)}, bf16[48,64,128]{2,1,0:T(8,128)(2,1)S(1)}, u32[]{:S(2)}) copy-start(bf16[48,64,128]{2,1,0:T(8,128)(2,1)S(1)} %pad_maximum_fusion.refs_0_) | copy-start | bytes 2359300
  21.6 25.1 %collective-permute-start.5 = (bf16[48,64,128]{2,1,0:T(8,128)(2,1)S(1)}, bf16[48,64,128]{2,1,0:T(8,128)(2,1)S(1)}, u32[]{:S(2)}, u32[]{:S(2)}) collective-permute-start(bf16[48,64,128]{2,1,0:T(8,128)(2,1)S(1)} %pad_maximum_fusion.refs_0_), channel_id=1, source_target_pairs={{0,128},{8,40},{16,144},{24,56},{32,160},{40,8},{48,176},{56,24},{... | collective-permute-start | bytes 2359304 | tf_op jit(solution)/shard_map/ppermute | solution.py:500
  24.4 22.3 %collective-permute-start.4 = (bf16[48,64,128]{2,1,0:T(8,128)(2,1)S(1)}, bf16[48,64,128]{2,1,0:T(8,128)(2,1)S(1)}, u32[]{:S(2)}, u32[]{:S(2)}) collective-permute-start(bf16[48,64,128]{2,1,0:T(8,128)(2,1)S(1)} %pad_maximum_fusion.refs_0_), channel_id=1, source_target_pairs={{0,192},{8,56},{16,208},{24,8},{32,224},{40,24},{48,240},{56,40},{... | collective-permute-start | bytes 2359304 | tf_op jit(solution)/shard_map/ppermute | solution.py:500
  25.3 21.5 %collective-permute-start.3 = (bf16[48,64,128]{2,1,0:T(8,128)(2,1)S(1)}, bf16[48,64,128]{2,1,0:T(8,128)(2,1)S(1)}, u32[]{:S(2)}, u32[]{:S(2)}) collective-permute-start(bf16[48,64,128]{2,1,0:T(8,128)(2,1)S(1)} %pad_maximum_fusion.refs_0_), channel_id=1, source_target_pairs={{0,64},{8,24},{16,80},{24,40},{32,96},{40,56},{48,112},{56,8},{64,... | collective-permute-start | bytes 2359304 | tf_op jit(solution)/shard_map/ppermute | solution.py:500
  25.9 21.6 %collective-permute-start.6 = (bf16[48,64,128]{2,1,0:T(8,128)(2,1)S(1)}, bf16[48,64,128]{2,1,0:T(8,128)(2,1)S(1)}, u32[]{:S(2)}, u32[]{:S(2)}) collective-permute-start(bf16[48,64,128]{2,1,0:T(8,128)(2,1)S(1)} %pad_maximum_fusion.refs_0_), channel_id=1, source_target_pairs={{0,8},{8,0},{16,24},{24,16},{32,40},{40,32},{48,56},{56,48},{64,72... | collective-permute-start | bytes 2359304 | tf_op jit(solution)/shard_map/ppermute | solution.py:504
  46.7 4.7 %copy-start.5 = (bf16[48,64,128]{2,1,0:T(8,128)(2,1)}, bf16[48,64,128]{2,1,0:T(8,128)(2,1)S(1)}, u32[]{:S(2)}) copy-start(bf16[48,64,128]{2,1,0:T(8,128)(2,1)S(1)} %collective-permute-done.5.refs_3_) | copy-start | bytes 2359300
  46.7 4.7 %copy-start.6 = (bf16[48,64,128]{2,1,0:T(8,128)(2,1)}, bf16[48,64,128]{2,1,0:T(8,128)(2,1)S(1)}, u32[]{:S(2)}) copy-start(bf16[48,64,128]{2,1,0:T(8,128)(2,1)S(1)} %collective-permute-done.4.refs_2_) | copy-start | bytes 2359300
  46.8 4.6 %copy-start.7 = (bf16[48,64,128]{2,1,0:T(8,128)(2,1)}, bf16[48,64,128]{2,1,0:T(8,128)(2,1)S(1)}, u32[]{:S(2)}) copy-start(bf16[48,64,128]{2,1,0:T(8,128)(2,1)S(1)} %collective-permute-done.3.refs_1_) | copy-start | bytes 2359300
  46.8 2.4 %collective-permute-start.7 = (bf16[48,64,128]{2,1,0:T(8,128)(2,1)S(1)}, bf16[48,64,128]{2,1,0:T(8,128)(2,1)S(1)}, u32[]{:S(2)}, u32[]{:S(2)}) collective-permute-start(bf16[48,64,128]{2,1,0:T(8,128)(2,1)S(1)} %collective-permute-done.3.refs_1_), channel_id=1, source_target_pairs={{0,8},{8,0},{16,24},{24,16},{32,40},{40,32},{48,56},{56,48},{64,72... | collective-permute-start | bytes 2359304 | tf_op jit(solution)/shard_map/ppermute | solution.py:504
  46.9 3.3 %collective-permute-start.8 = (bf16[48,64,128]{2,1,0:T(8,128)(2,1)S(1)}, bf16[48,64,128]{2,1,0:T(8,128)(2,1)S(1)}, u32[]{:S(2)}, u32[]{:S(2)}) collective-permute-start(bf16[48,64,128]{2,1,0:T(8,128)(2,1)S(1)} %collective-permute-done.4.refs_2_), channel_id=1, source_target_pairs={{0,8},{8,0},{16,24},{24,16},{32,40},{40,32},{48,56},{56,48},{64,72... | collective-permute-start | bytes 2359304 | tf_op jit(solution)/shard_map/ppermute | solution.py:504
  47.4 4.0 %collective-permute-start.9 = (bf16[48,64,128]{2,1,0:T(8,128)(2,1)S(1)}, bf16[48,64,128]{2,1,0:T(8,128)(2,1)S(1)}, u32[]{:S(2)}, u32[]{:S(2)}) collective-permute-start(bf16[48,64,128]{2,1,0:T(8,128)(2,1)S(1)} %collective-permute-done.5.refs_3_), channel_id=1, source_target_pairs={{0,8},{8,0},{16,24},{24,16},{32,40},{40,32},{48,56},{56,48},{64,72... | collective-permute-start | bytes 2359304 | tf_op jit(solution)/shard_map/ppermute | solution.py:504
  47.5 3.9 %copy-start.8 = (bf16[48,64,128]{2,1,0:T(8,128)(2,1)}, bf16[48,64,128]{2,1,0:T(8,128)(2,1)S(1)}, u32[]{:S(2)}) copy-start(bf16[48,64,128]{2,1,0:T(8,128)(2,1)S(1)} %collective-permute-done.6.refs_4_) | copy-start | bytes 2359300
  49.1 2.3 %copy-start.9 = (bf16[48,64,128]{2,1,0:T(8,128)(2,1)}, bf16[48,64,128]{2,1,0:T(8,128)(2,1)S(1)}, u32[]{:S(2)}) copy-start(bf16[48,64,128]{2,1,0:T(8,128)(2,1)S(1)} %collective-permute-done.7.refs_5_) | copy-start | bytes 2359300
  50.3 1.2 copy-start.10
  51.4 0.9 copy-start.11

commit v4 on v3

--- a/solution.py
+++ b/solution.py
@@ -44,24 +44,12 @@
     return jnp.where(is_low, k, jnp.minimum(high_block, 11) + 1)
 
 
-def butterfly(parts, lane):
-    parts = list(parts)
+def exchange(parts, lane):
+    parts = [parts[-g % 32] for g in range(32)]
     for bit in range(5):
-        distance = 4 << bit
-        upper = (lane & distance) != 0
-        for low in range(32):
-            if low & (1 << bit):
-                continue
-            high = low | (1 << bit)
-            first, second = parts[low], parts[high]
-            if distance == 64:
-                swapped = pltpu.roll(jnp.where(upper, first, second), 64, 1)
-                parts[low] = jnp.where(upper, swapped, first)
-                parts[high] = jnp.where(upper, second, swapped)
-                continue
-            parts[low] = jnp.where(upper, pltpu.roll(second, distance, 1), first)
-            parts[high] = jnp.where(upper, second, pltpu.roll(first, 128 - distance, 1))
-    return parts
+        upper = (lane & (4 << bit)) != 0
+        parts = [jnp.where(upper, parts[(g - (1 << bit)) % 32], parts[g]) for g in range(32)]
+    return [pltpu.roll(parts[g], -4 * g % 128, 1) if g else parts[g] for g in range(32)]
 
 
 def coeff_kernel(e_ref, first_ref, second_ref, out_ref):
@@ -80,24 +68,27 @@
                     c, sub = divmod(2 * tile + half, 3)
                     a = first_ref[c, n].astype(F32)[8 * sub : 8 * sub + 8]
                     b = second_ref[c, n].astype(F32)[8 * sub : 8 * sub + 8]
-                    halves.append(shifted(a, b, sub))
+                    halves.append(shifted(a, b, sub, n))
                 parts.append(jnp.concatenate(halves, axis=0).astype(BF))
-            parts = butterfly(parts, lane)
+            parts = exchange(parts, lane)
             for g in range(GROUPS):
                 out_ref[0, g, 16 * tile : 16 * tile + 16, :] = parts[g]
 
     @pl.when(is_low)
     def _():
-        def shifted(a, b, sub):
+        def shifted(a, b, sub, n):
             mixed = jnp.where(lane8 < 128 - 8 * sub - row8, b, a)
-            return pltpu.roll(mixed, 8 * sub, 1, stride=1, stride_axis=0)
+            base = (8 * sub + 4 * n) % 128
+            if base > 120:
+                return pltpu.roll(pltpu.roll(mixed, base - 64, 1, stride=1, stride_axis=0), 64, 1)
+            return pltpu.roll(mixed, base, 1, stride=1, stride_axis=0)
 
         run(shifted)
 
     @pl.when(jnp.logical_not(is_low))
     def _():
-        def shifted(a, b, sub):
-            return pltpu.roll(jnp.where(lane8 >= 1, a, b), 127, 1)
+        def shifted(a, b, sub, n):
+            return pltpu.roll(jnp.where(lane8 >= 1, a, b), (127 + 4 * n) % 128, 1)
 
         run(shifted)
 
@@ -360,7 +351,7 @@
     )(e, twist, coeffs, *gathered, angular)
 
 
-SOURCES_STEP = 8
+SOURCES_STEP = 16
 
 
 def pixels_kernel(in_ref, basis_ref, dens_ref, disp_ref, total):
@@ -454,7 +445,7 @@
         parts = [
             stage[pl.ds(owner * 8 * ROW_PITCH + n, 8, stride=ROW_PITCH), :] for n in range(MODES_DEV)
         ]
-        parts = butterfly(parts, lane)
+        parts = exchange([pltpu.roll(x, 4 * n, 1) if n else x for n, x in enumerate(parts)], lane)
         for g in range(width // 4):
             grouped[g, pl.ds(pl.multiple_of(owner * 8, 8), 8), :] = parts[g]
         return carry

time: 121 us -> 118 us (0.975)
  Pallas kernels: 61 us -> 50.8 us
  waiting for transfers between devices: 3.93 us -> 7.93 us
  starting transfers between devices: 12.6 us -> 15 us
    pallas_call x1, Pallas kernels: 18.5 us -> 10.3 us  [coeff_blocks(): pl.pallas_call(coeff_kernel, out_shape=jax.ShapeDtypeStruct((STEPS, GROUP...]
    ppermute x6, waiting for transfers between devices: 0.02 us -> 4.29 us  [ring_shift(): return lax.ppermute(value, 'ell', pairs)]
    ppermute x4, starting transfers between devices: 3.04 us -> 5.39 us  [other_core(): return lax.ppermute(value, 'ell', [(e, e ^ 1) for e in range(32)])]
  transfers between devices with their start and end apart: 10 -> 10, of which waited for: 3 -> 4; matrix products, arithmetic and copies ran while one was open for 0% -> 0% of each run, Pallas kernels for 23% -> 17%
where the time goes in v4:
time: 118 us
  Pallas kernels  50.8 us (43%)
  blocking collectives  38.7 us (33%)
  starting transfers between devices  15 us (13%)
  waiting for transfers between devices  7.93 us (7%)
  local copies, waits for them, and re-layouts  4.46 us (4%)
    all_to_all x1, blocking collectives, local(): lax.all_to_all(sums.reshape(256, 4, 384), ('rad', 'ell'), split_axis=0, c...  38.7 us
    pallas_call x1, Pallas kernels, cycle_sums(): pl.pallas_call(sums_kernel, out_shape=jax.ShapeDtypeStruct((8, 32, 4, 384...  25.4 us
    pallas_call x1, Pallas kernels, coeff_blocks(): pl.pallas_call(coeff_kernel, out_shape=jax.ShapeDtypeStruct((STEPS, GROUP...  10.3 us
    pallas_call x1, Pallas kernels, angular_blocks(): pl.pallas_call(angular_kernel, out_shape=jax.ShapeDtypeStruct((PAIR_DEV,...  9.79 us
    ppermute x6, starting transfers between devices, ring_shift(): return lax.ppermute(value, 'ell', pairs)  9.59 us
    ppermute x4, starting transfers between devices, other_core(): return lax.ppermute(value, 'ell', [(e, e ^ 1) for e in range(32)])  5.39 us
    unnamed x28, local copies, waits for them, and re-layouts  4.38 us
    pallas_call x1, Pallas kernels, pixels(): pl.pallas_call(pixels_kernel, out_shape=(out, out), grid=(32 // SOURCES_S...  4.37 us
  transfers between devices with their start and end apart: 10, of which 4 were waited for; matrix products, arithmetic and copies ran while one was open for 0% of the time, Pallas kernels for 17%

profile of v4, /device:TPU:1, one launch (start us, length us, event | category | flops | bytes accessed | tf_op | source)
XLA Modules:
  0.0 117.8 jit_solution(3922541384418075659)
XLA Ops:
  0.6 0.0 copy-start
  0.7 0.7 copy-done
  1.3 0.1 dynamic-slice_bitcast_fusion.counts_ref
  1.4 0.0 copy-start.3
  1.4 1.0 copy-done.3
  2.5 0.0 slice-start
  2.5 0.9 radial_table.1
  3.4 3.8 %collective-permute-start.2 = (bf16[12,64,128]{2,1,0:T(8,128)(2,1)S(1)}, bf16[12,64,128]{2,1,0:T(8,128)(2,1)S(1)}, u32[]{:S(2)}, u32[]{:S(2)}) collective-permute-start(bf16[12,64,128]{2,1,0:T(8,128)(2,1)S(1)} %radial_table.1), channel_id=1, source_target_pairs={{0,32},{8,136},{16,48},{24,152},{32,0},{40,168},{48,16},{56,184},{... | collective-permute-start | bytes 589832 | tf_op jit(solution)/shard_map/ppermute | solution.py:491
  7.2 0.8 collective-permute-start.1
  8.0 0.7 collective-permute-start
  8.7 0.0 copy-start.2
  8.7 1.7 %copy-done.2 = bf16[32,24,1537]{2,1,0:T(8,128)(2,1)S(1)} copy-done((bf16[32,24,1537]{2,1,0:T(8,128)(2,1)S(1)}, bf16[32,24,1537]{2,1,0:T(8,128)(2,1)}, u32[]{:S(2)}) %copy-start.2) | copy-done | bytes 2360856
  10.4 0.0 slice-start.1
  10.4 9.8 %angular_blocks.1.refs_8_ = bf16[24,128,512]{2,1,0:T(8,128)(2,1)S(1)} custom-call(s32[1]{0:T(128)} %bitcast.e_ref, bf16[32,24,1537]{2,1,0:T(8,128)(2,1)S(1)} %copy-done.2, bf16[32,24,1537]{2,1,0:T(8,128)(2,1)S(1)} %copy-done.2), custom_call_target="tpu_custom_call" | custom-call | tf_op jit(solution)/shard_map/angular_blocks/pallas_call | solution.py:179
  20.2 0.0 copy-start.1
  20.2 0.0 collective-permute-done.2
  20.3 0.0 collective-permute-done.1
  20.3 0.0 collective-permute-done
  20.3 0.1 pad_maximum_fusion.refs_0_
  20.4 0.0 copy-start.4
  20.4 2.8 %collective-permute-start.5 = (bf16[48,64,128]{2,1,0:T(8,128)(2,1)S(1)}, bf16[48,64,128]{2,1,0:T(8,128)(2,1)S(1)}, u32[]{:S(2)}, u32[]{:S(2)}) collective-permute-start(bf16[48,64,128]{2,1,0:T(8,128)(2,1)S(1)} %pad_maximum_fusion.refs_0_), channel_id=1, source_target_pairs={{0,128},{8,40},{16,144},{24,56},{32,160},{40,8},{48,176},{56,24},{... | collective-permute-start | bytes 2359304 | tf_op jit(solution)/shard_map/ppermute | solution.py:491
  23.2 0.9 collective-permute-start.4
  24.1 0.6 collective-permute-start.3
  24.7 2.4 %collective-permute-start.6 = (bf16[48,64,128]{2,1,0:T(8,128)(2,1)S(1)}, bf16[48,64,128]{2,1,0:T(8,128)(2,1)S(1)}, u32[]{:S(2)}, u32[]{:S(2)}) collective-permute-start(bf16[48,64,128]{2,1,0:T(8,128)(2,1)S(1)} %pad_maximum_fusion.refs_0_), channel_id=1, source_target_pairs={{0,8},{8,0},{16,24},{24,16},{32,40},{40,32},{48,56},{56,48},{64,72... | collective-permute-start | bytes 2359304 | tf_op jit(solution)/shard_map/ppermute | solution.py:495
  27.0 0.0 slice-done
  27.0 0.0 slice-done.1
  27.0 10.3 %coeff_blocks.1.coeff_ref = bf16[14,32,48,128]{3,2,1,0:T(8,128)(2,1)} custom-call(s32[1]{0:T(128)} %bitcast.e_ref, bf16[2,32,24,1537]{3,2,1,0:T(8,128)(2,1)S(1)} %bitcast.7, bf16[2,32,24,1537]{3,2,1,0:T(8,128)(2,1)S(1)} %bitcast.7), custom_call_target="tpu_custom_call" | custom-call | tf_op jit(solution)/shard_map/coeff_blocks/pallas_call | solution.py:98
  37.4 0.0 copy-done.1
  37.4 0.0 copy-done.4
  37.4 0.0 collective-permute-done.5.refs_3_
  37.4 0.0 copy-start.5
  37.4 4.3 %collective-permute-done.4.refs_2_ = bf16[48,64,128]{2,1,0:T(8,128)(2,1)S(1)} collective-permute-done((bf16[48,64,128]{2,1,0:T(8,128)(2,1)S(1)}, bf16[48,64,128]{2,1,0:T(8,128)(2,1)S(1)}, u32[]{:S(2)}, u32[]{:S(2)}) %collective-permute-start.4) | collective-permute-done | bytes 786464 | tf_op jit(solution)/shard_map/ppermute | solution.py:491
  41.7 0.0 copy-start.6
  41.7 0.0 collective-permute-done.3.refs_1_
  41.7 0.0 copy-start.7
  41.7 2.5 %collective-permute-start.7 = (bf16[48,64,128]{2,1,0:T(8,128)(2,1)S(1)}, bf16[48,64,128]{2,1,0:T(8,128)(2,1)S(1)}, u32[]{:S(2)}, u32[]{:S(2)}) collective-permute-start(bf16[48,64,128]{2,1,0:T(8,128)(2,1)S(1)} %collective-permute-done.3.refs_1_), channel_id=1, source_target_pairs={{0,8},{8,0},{16,24},{24,16},{32,40},{40,32},{48,56},{56,48},{64,72... | collective-permute-start | bytes 2359304 | tf_op jit(solution)/shard_map/ppermute | solution.py:495
  44.2 0.1 collective-permute-start.8
  44.3 0.4 collective-permute-start.9
  44.7 0.0 collective-permute-done.6.refs_4_
  44.7 0.0 copy-start.8
  44.7 1.4 %collective-permute-done.7.refs_5_ = bf16[48,64,128]{2,1,0:T(8,128)(2,1)S(1)} collective-permute-done((bf16[48,64,128]{2,1,0:T(8,128)(2,1)S(1)}, bf16[48,64,128]{2,1,0:T(8,128)(2,1)S(1)}, u32[]{:S(2)}, u32[]{:S(2)}) %collective-permute-start.7) | collective-permute-done | bytes 786464 | tf_op jit(solution)/shard_map/ppermute | solution.py:495
  46.1 0.0 copy-start.9
  46.1 1.1 collective-permute-done.8.refs_6_
  47.2 0.0 copy-start.10
  47.2 1.1 collective-permute-done.9.refs_7_
  48.4 0.0 copy-done.5
  48.4 0.0 copy-done.6
  48.4 0.0 copy-done.7
  48.4 0.0 copy-done.8
  48.4 0.0 copy-done.9
  48.4 0.0 copy-done.10
  48.4 0.0 copy-start.11
  48.4 0.9 copy-done.11
  49.3 25.4 %cycle_sums.1 = bf16[8,32,4,384]{3,2,1,0:T(4,128)(2,1)} custom-call(s32[1]{0:T(128)} %bitcast.e_ref, f32[96,48]{1,0:T(8,128)} %constant.19.clone.twist_ref, bf16[14,32,48,128]{3,2,1,0:T(8,128)(2,1)} %coeff_blocks.1.coeff_ref, bf16[48,64,128]{2,1,0:T(8,128)(2,1)} %copy-done.4, bf16[48,64,128]{2,1,0:T(8,128)(2,1)} %copy-done.7, ...), custom_call_target="tpu_custom_call" | custom-call | tf_op jit(solution)/shard_map/cycle_sums/pallas_call | solution.py:328
  74.7 38.7 %all_to_all.5 = bf16[256,4,384]{2,1,0:T(4,128)(2,1)S(1)} all-to-all(bf16[256,4,384]{2,1,0:T(4,128)(2,1)} %bitcast.9), channel_id=1, replica_groups=mesh['ell'=32,'rad'=8] {'rad','ell'}, dimensions={0} | all-to-all | bytes 1572864 | tf_op jit(solution)/shard_map/all_to_all | solution.py:522
  113.4 4.4 %pixels.1 = (f32[4,2,2048]{2,1,0:T(2,128)}, f32[4,2,2048]{2,1,0:T(2,128)}) custom-call(bf16[8,32,4,384]{3,2,1,0:T(4,128)(2,1)S(1)} %bitcast.8, bf16[32,96,1024]{2,1,0:T(8,128)(2,1)} %constant.20.clone.basis_ref), custom_call_target="tpu_custom_call" | custom-call | tf_op jit(solution)/shard_map/pixels/pallas_call | solution.py:417
  (1 shorter events, 0.0 us)
Async XLA Ops:
  0.6 0.7 copy-start
  1.4 1.0 copy-start.3
  2.5 24.6 %slice-start = ((s8[5111808]{0:T(1024)(128)(4,1)}), s8[4194304]{0:T(1024)(128)(4,1)S(1)}, s32[]{:S(2)}) async-start(s8[5111808]{0:T(1024)(128)(4,1)} %bitcast.6), calls=%async_computation.1 | async-start | bytes 8388608
  3.4 16.8 %collective-permute-start.2 = (bf16[12,64,128]{2,1,0:T(8,128)(2,1)S(1)}, bf16[12,64,128]{2,1,0:T(8,128)(2,1)S(1)}, u32[]{:S(2)}, u32[]{:S(2)}) collective-permute-start(bf16[12,64,128]{2,1,0:T(8,128)(2,1)S(1)} %radial_table.1), channel_id=1, source_target_pairs={{0,32},{8,136},{16,48},{24,152},{32,0},{40,168},{48,16},{56,184},{... | collective-permute-start | bytes 589832 | tf_op jit(solution)/shard_map/ppermute | solution.py:491
  7.2 13.0 %collective-permute-start.1 = (bf16[12,64,128]{2,1,0:T(8,128)(2,1)S(1)}, bf16[12,64,128]{2,1,0:T(8,128)(2,1)S(1)}, u32[]{:S(2)}, u32[]{:S(2)}) collective-permute-start(bf16[12,64,128]{2,1,0:T(8,128)(2,1)S(1)} %radial_table.1), channel_id=1, source_target_pairs={{0,48},{8,200},{16,0},{24,216},{32,16},{40,232},{48,32},{56,248},{... | collective-permute-start | bytes 589832 | tf_op jit(solution)/shard_map/ppermute | solution.py:491
  8.0 12.3 %collective-permute-start = (bf16[12,64,128]{2,1,0:T(8,128)(2,1)S(1)}, bf16[12,64,128]{2,1,0:T(8,128)(2,1)S(1)}, u32[]{:S(2)}, u32[]{:S(2)}) collective-permute-start(bf16[12,64,128]{2,1,0:T(8,128)(2,1)S(1)} %radial_table.1), channel_id=1, source_target_pairs={{0,16},{8,72},{16,32},{24,88},{32,48},{40,104},{48,0},{56,120},{64... | collective-permute-start | bytes 589832 | tf_op jit(solution)/shard_map/ppermute | solution.py:491
  8.7 1.7 %copy-start.2 = (bf16[32,24,1537]{2,1,0:T(8,128)(2,1)S(1)}, bf16[32,24,1537]{2,1,0:T(8,128)(2,1)}, u32[]{:S(2)}) copy-start(bf16[32,24,1537]{2,1,0:T(8,128)(2,1)} %second_ref.2) | copy-start | bytes 7082500
  10.4 16.6 %slice-start.1 = ((s8[5111808]{0:T(1024)(128)(4,1)}), s8[917504]{0:T(1024)(128)(4,1)S(1)}, s32[]{:S(2)}) async-start(s8[5111808]{0:T(1024)(128)(4,1)} %bitcast.6), calls=%async_computation.2 | async-start | bytes 1835008
  20.2 17.1 %copy-start.1 = (bf16[24,128,512]{2,1,0:T(8,128)(2,1)}, bf16[24,128,512]{2,1,0:T(8,128)(2,1)S(1)}, u32[]{:S(2)}) copy-start(bf16[24,128,512]{2,1,0:T(8,128)(2,1)S(1)} %angular_blocks.1.refs_8_) | copy-start | bytes 9437188
  20.4 17.0 %copy-start.4 = (bf16[48,64,128]{2,1,0:T(8,128)(2,1)}, bf16[48,64,128]{2,1,0:T(8,128)(2,1)S(1)}, u32[]{:S(2)}) copy-start(bf16[48,64,128]{2,1,0:T(8,128)(2,1)S(1)} %pad_maximum_fusion.refs_0_) | copy-start | bytes 2359300
  20.4 17.0 %collective-permute-start.5 = (bf16[48,64,128]{2,1,0:T(8,128)(2,1)S(1)}, bf16[48,64,128]{2,1,0:T(8,128)(2,1)S(1)}, u32[]{:S(2)}, u32[]{:S(2)}) collective-permute-start(bf16[48,64,128]{2,1,0:T(8,128)(2,1)S(1)} %pad_maximum_fusion.refs_0_), channel_id=1, source_target_pairs={{0,128},{8,40},{16,144},{24,56},{32,160},{40,8},{48,176},{56,24},{... | collective-permute-start | bytes 2359304 | tf_op jit(solution)/shard_map/ppermute | solution.py:491
  23.2 18.5 %collective-permute-start.4 = (bf16[48,64,128]{2,1,0:T(8,128)(2,1)S(1)}, bf16[48,64,128]{2,1,0:T(8,128)(2,1)S(1)}, u32[]{:S(2)}, u32[]{:S(2)}) collective-permute-start(bf16[48,64,128]{2,1,0:T(8,128)(2,1)S(1)} %pad_maximum_fusion.refs_0_), channel_id=1, source_target_pairs={{0,192},{8,56},{16,208},{24,8},{32,224},{40,24},{48,240},{56,40},{... | collective-permute-start | bytes 2359304 | tf_op jit(solution)/shard_map/ppermute | solution.py:491
  24.1 17.6 %collective-permute-start.3 = (bf16[48,64,128]{2,1,0:T(8,128)(2,1)S(1)}, bf16[48,64,128]{2,1,0:T(8,128)(2,1)S(1)}, u32[]{:S(2)}, u32[]{:S(2)}) collective-permute-start(bf16[48,64,128]{2,1,0:T(8,128)(2,1)S(1)} %pad_maximum_fusion.refs_0_), channel_id=1, source_target_pairs={{0,64},{8,24},{16,80},{24,40},{32,96},{40,56},{48,112},{56,8},{64,... | collective-permute-start | bytes 2359304 | tf_op jit(solution)/shard_map/ppermute | solution.py:491
  24.7 20.0 %collective-permute-start.6 = (bf16[48,64,128]{2,1,0:T(8,128)(2,1)S(1)}, bf16[48,64,128]{2,1,0:T(8,128)(2,1)S(1)}, u32[]{:S(2)}, u32[]{:S(2)}) collective-permute-start(bf16[48,64,128]{2,1,0:T(8,128)(2,1)S(1)} %pad_maximum_fusion.refs_0_), channel_id=1, source_target_pairs={{0,8},{8,0},{16,24},{24,16},{32,40},{40,32},{48,56},{56,48},{64,72... | collective-permute-start | bytes 2359304 | tf_op jit(solution)/shard_map/ppermute | solution.py:495
  37.4 11.0 %copy-start.5 = (bf16[48,64,128]{2,1,0:T(8,128)(2,1)}, bf16[48,64,128]{2,1,0:T(8,128)(2,1)S(1)}, u32[]{:S(2)}) copy-start(bf16[48,64,128]{2,1,0:T(8,128)(2,1)S(1)} %collective-permute-done.5.refs_3_) | copy-start | bytes 2359300
  41.7 6.7 %copy-start.6 = (bf16[48,64,128]{2,1,0:T(8,128)(2,1)}, bf16[48,64,128]{2,1,0:T(8,128)(2,1)S(1)}, u32[]{:S(2)}) copy-start(bf16[48,64,128]{2,1,0:T(8,128)(2,1)S(1)} %collective-permute-done.4.refs_2_) | copy-start | bytes 2359300
  41.7 6.7 %copy-start.7 = (bf16[48,64,128]{2,1,0:T(8,128)(2,1)}, bf16[48,64,128]{2,1,0:T(8,128)(2,1)S(1)}, u32[]{:S(2)}) copy-start(bf16[48,64,128]{2,1,0:T(8,128)(2,1)S(1)} %collective-permute-done.3.refs_1_) | copy-start | bytes 2359300
  41.7 4.4 %collective-permute-start.7 = (bf16[48,64,128]{2,1,0:T(8,128)(2,1)S(1)}, bf16[48,64,128]{2,1,0:T(8,128)(2,1)S(1)}, u32[]{:S(2)}, u32[]{:S(2)}) collective-permute-start(bf16[48,64,128]{2,1,0:T(8,128)(2,1)S(1)} %collective-permute-done.3.refs_1_), channel_id=1, source_target_pairs={{0,8},{8,0},{16,24},{24,16},{32,40},{40,32},{48,56},{56,48},{64,72... | collective-permute-start | bytes 2359304 | tf_op jit(solution)/shard_map/ppermute | solution.py:495
  44.2 3.0 %collective-permute-start.8 = (bf16[48,64,128]{2,1,0:T(8,128)(2,1)S(1)}, bf16[48,64,128]{2,1,0:T(8,128)(2,1)S(1)}, u32[]{:S(2)}, u32[]{:S(2)}) collective-permute-start(bf16[48,64,128]{2,1,0:T(8,128)(2,1)S(1)} %collective-permute-done.4.refs_2_), channel_id=1, source_target_pairs={{0,8},{8,0},{16,24},{24,16},{32,40},{40,32},{48,56},{56,48},{64,72... | collective-permute-start | bytes 2359304 | tf_op jit(solution)/shard_map/ppermute | solution.py:495
  44.3 4.1 %collective-permute-start.9 = (bf16[48,64,128]{2,1,0:T(8,128)(2,1)S(1)}, bf16[48,64,128]{2,1,0:T(8,128)(2,1)S(1)}, u32[]{:S(2)}, u32[]{:S(2)}) collective-permute-start(bf16[48,64,128]{2,1,0:T(8,128)(2,1)S(1)} %collective-permute-done.5.refs_3_), channel_id=1, source_target_pairs={{0,8},{8,0},{16,24},{24,16},{32,40},{40,32},{48,56},{56,48},{64,72... | collective-permute-start | bytes 2359304 | tf_op jit(solution)/shard_map/ppermute | solution.py:495
  44.7 3.7 %copy-start.8 = (bf16[48,64,128]{2,1,0:T(8,128)(2,1)}, bf16[48,64,128]{2,1,0:T(8,128)(2,1)S(1)}, u32[]{:S(2)}) copy-start(bf16[48,64,128]{2,1,0:T(8,128)(2,1)S(1)} %collective-permute-done.6.refs_4_) | copy-start | bytes 2359300
  46.1 2.3 %copy-start.9 = (bf16[48,64,128]{2,1,0:T(8,128)(2,1)}, bf16[48,64,128]{2,1,0:T(8,128)(2,1)S(1)}, u32[]{:S(2)}) copy-start(bf16[48,64,128]{2,1,0:T(8,128)(2,1)S(1)} %collective-permute-done.7.refs_5_) | copy-start | bytes 2359300
  47.2 1.1 copy-start.10
  48.4 0.9 copy-start.11

commit v5 on v4

--- a/solution.py
+++ b/solution.py
@@ -21,6 +21,7 @@
 ROW_PITCH = 40
 PIECE = 12
 SHIFTS = (0, 1, -1, 2)
+ANGULAR_PARTS = ((0, 2), (2, 1), (3, 1))
 BF = jnp.bfloat16
 F32 = jnp.float32
 
@@ -112,13 +113,13 @@
     )(e, coefficients, coefficients)
 
 
-def angular_kernel(e_ref, first_ref, second_ref, out_ref, stage, wide, pick_ref):
-    k = pl.program_id(0)
+def angular_kernel(start, e_ref, first_ref, second_ref, out_ref, stage, wide, pick_ref):
+    k = pl.program_id(0) + start
     e = e_ref[0]
     p0, _, is_low, high_block = step_info(k, e)
     quarter = k % 4
 
-    @pl.when(k == 0)
+    @pl.when(k == start)
     def _():
         slot = lax.broadcasted_iota(jnp.int32, (512, 128), 0)
         column = lax.broadcasted_iota(jnp.int32, (512, 128), 1)
@@ -174,20 +175,29 @@
                 out_ref[i, 32 * j : 32 * j + 32, :] = picked[32 * i : 32 * i + 32].astype(BF)
 
 
-def angular_blocks(e, legendre):
+def angular_blocks(e, legendre, first_quad, quads):
     block = (32, PAIR_DEV, 128)
+    start = 4 * first_quad
     return pl.pallas_call(
-        angular_kernel,
-        out_shape=jax.ShapeDtypeStruct((PAIR_DEV, 128, KPAD), BF),
+        functools.partial(angular_kernel, start),
+        out_shape=jax.ShapeDtypeStruct((PAIR_DEV, 128, 128 * quads), BF),
         grid_spec=pltpu.PrefetchScalarGridSpec(
             num_scalar_prefetch=1,
-            grid=(16,),
+            grid=(4 * quads,),
             in_specs=[
-                pl.BlockSpec(block, lambda k, s: (0, 0, window_low(jnp.minimum(k, STEPS - 1), s[0]))),
-                pl.BlockSpec(block, lambda k, s: (0, 0, window_high(jnp.minimum(k, STEPS - 1), s[0]))),
+                pl.BlockSpec(
+                    block, lambda k, s: (0, 0, window_low(jnp.minimum(k + start, STEPS - 1), s[0]))
+                ),
+                pl.BlockSpec(
+                    block, lambda k, s: (0, 0, window_high(jnp.minimum(k + start, STEPS - 1), s[0]))
+                ),
             ],
             out_specs=pl.BlockSpec((PAIR_DEV, 128, 128), lambda k, s: (0, 0, k // 4)),
-            scratch_shapes=[pltpu.VMEM((PAIR_DEV * ROW_PITCH, 128), F32), pltpu.VMEM((PAIR_DEV * 32, 512), BF), pltpu.VMEM((512, 512), BF)],
+            scratch_shapes=[
+                pltpu.VMEM((PAIR_DEV * ROW_PITCH, 128), F32),
+                pltpu.VMEM((PAIR_DEV * 32, 512), BF),
+                pltpu.VMEM((512, 512), BF),
+            ],
         ),
         compiler_params=pltpu.CompilerParams(vmem_limit_bytes=48 * 2**20),
         name="angular_blocks",
@@ -208,12 +218,16 @@
 
 
 def sums_kernel(e_ref, twist_ref, coeff_ref, *refs):
-    gathered, (angular_hbm, out_ref, left, right, turned, table_ref, angular_ref, sems, sem) = refs[:8], refs[8:]
+    gathered, angular, refs = refs[:8], refs[8:11], refs[11:]
+    out_ref, left, right, turned, table_ref, angular_ref, sems, angular_sems = refs
     k = pl.program_id(0)
     e = e_ref[0]
     p0, n_low, _, _ = step_info(k, e)
     base = table_first(k, e)
-    fetch = pltpu.make_async_copy(angular_hbm, angular_ref, sem)
+    fetches = []
+    for part, (first_quad, quads) in enumerate(ANGULAR_PARTS):
+        place = angular_ref.at[:, :, pl.ds(128 * first_quad, 128 * quads)]
+        fetches.append(pltpu.make_async_copy(angular[part], place, angular_sems.at[part]))
     first_piece = p0 // 4 // PIECE
 
     @pl.when(k == 0)
@@ -231,7 +245,8 @@
                         sems.at[owner],
                     ).start()
 
-        fetch.start()
+        for fetch in fetches:
+            fetch.start()
 
     last_group = L // 4 - 1
     wait_from = jnp.where(
@@ -268,7 +283,8 @@
 
     @pl.when(k == STEPS - 1)
     def _():
-        fetch.wait()
+        for fetch in fetches:
+            fetch.wait()
         slot = lax.broadcasted_iota(jnp.int32, (64, SPAN), 1)
         low_slot = slot < GROUPS * n_low
         near = lax.broadcasted_iota(jnp.int32, (32, 128), 1) < 64
@@ -333,7 +349,7 @@
             grid=(STEPS,),
             in_specs=[
                 pl.BlockSpec((1, GROUPS, 48, 128), lambda k, s, t: (k, 0, 0, 0)),
-                *[pl.BlockSpec(memory_space=pl.ANY)] * 9,
+                *[pl.BlockSpec(memory_space=pl.ANY)] * 11,
             ],
             out_specs=pl.BlockSpec((8, 32, 4, 384), lambda k, s, t: (0, 0, 0, 0)),
             scratch_shapes=[
@@ -343,12 +359,12 @@
                 pltpu.VMEM((L // 4, 64, 128), BF),
                 pltpu.VMEM((PAIR_DEV, 128, KPAD), BF),
                 pltpu.SemaphoreType.DMA((32,)),
-                pltpu.SemaphoreType.DMA,
+                pltpu.SemaphoreType.DMA((3,)),
             ],
         ),
         compiler_params=pltpu.CompilerParams(vmem_limit_bytes=56 * 2**20),
         name="cycle_sums",
-    )(e, twist, coeffs, *gathered, angular)
+    )(e, twist, coeffs, *gathered, *angular)
 
 
 SOURCES_STEP = 16
@@ -509,15 +525,21 @@
     twist = jnp.asarray(twist_table())
     table = radial_table(bessel, mode_counts)
     moved = [ring_shift(table, shift, True) for shift in SHIFTS[1:]]
-    angular = angular_blocks(e_arr, legendre)
-    angular, *moved = lax.optimization_barrier((angular, *moved))
+    early = angular_blocks(e_arr, legendre, *ANGULAR_PARTS[0])
+    early, *moved = lax.optimization_barrier((early, *moved))
     own = jnp.concatenate([table, *moved], axis=0)
     far = [ring_shift(own, shift, False) for shift in SHIFTS[1:]]
     e_late, own = lax.optimization_barrier((e_arr, own))
     coeffs = coeff_blocks(e_late, coefficients)
-    coeffs, *far = lax.optimization_barrier((coeffs, *far))
+    middle = angular_blocks(e_late, legendre, *ANGULAR_PARTS[1])
+    coeffs, middle, *far = lax.optimization_barrier((coeffs, middle, *far))
     mine = [own, *far]
-    gathered = mine + [other_core(value) for value in mine]
+    theirs = [other_core(value) for value in mine]
+    e_last, *far = lax.optimization_barrier((e_arr, *far))
+    late = angular_blocks(e_last, legendre, *ANGULAR_PARTS[2])
+    late, *theirs = lax.optimization_barrier((late, *theirs))
+    gathered = mine + theirs
+    angular = (early, middle, late)
     sums = cycle_sums(e_arr, twist, coeffs, gathered, angular)
     received = lax.all_to_all(
         sums.reshape(256, 4, 384), ("rad", "ell"), split_axis=0, concat_axis=0, tiled=True

time: 118 us -> 116 us (0.983)
  waiting for transfers between devices: 7.93 us -> 1.59 us
  local copies, waits for them, and re-layouts: 4.46 us -> 8.29 us
    unnamed x28 -> x32, local copies, waits for them, and re-layouts: 4.38 us -> 8.21 us
    ppermute x4, waiting for transfers between devices: 3.64 us -> 0.01 us  [other_core(): return lax.ppermute(value, 'ell', [(e, e ^ 1) for e in range(32)])]
    ppermute x6, waiting for transfers between devices: 4.29 us -> 1.58 us  [ring_shift(): return lax.ppermute(value, 'ell', pairs)]
    pallas_call x1 -> x3, Pallas kernels: 9.79 us -> 9.94 us  [angular_blocks(): pl.pallas_call(functools.partial(angular_kernel, start), out_shape=jax.Sh...]
  transfers between devices with their start and end apart: 10 -> 10, of which waited for: 4 -> 1; matrix products, arithmetic and copies ran while one was open for 0% -> 0% of each run, Pallas kernels for 17% -> 18%
where the time goes in v5:
time: 116 us; the launch traced here: 115 us
  Pallas kernels  51 us (44%)
  blocking collectives  38.3 us (33%)
  starting transfers between devices  15.1 us (13%)
  local copies, waits for them, and re-layouts  8.29 us (7%)
  waiting for transfers between devices  1.59 us (1%)
    all_to_all x1, blocking collectives, local(): lax.all_to_all(sums.reshape(256, 4, 384), ('rad', 'ell'), split_axis=0, c...  38.3 us
    pallas_call x1, Pallas kernels, cycle_sums(): pl.pallas_call(sums_kernel, out_shape=jax.ShapeDtypeStruct((8, 32, 4, 384...  25.4 us
    pallas_call x1, Pallas kernels, coeff_blocks(): pl.pallas_call(coeff_kernel, out_shape=jax.ShapeDtypeStruct((STEPS, GROUP...  10.3 us
    pallas_call x3, Pallas kernels, angular_blocks(): pl.pallas_call(functools.partial(angular_kernel, start), out_shape=jax.Sh...  9.94 us
    ppermute x6, starting transfers between devices, ring_shift(): return lax.ppermute(value, 'ell', pairs)  9.6 us
    unnamed x32, local copies, waits for them, and re-layouts  8.21 us
    ppermute x4, starting transfers between devices, other_core(): return lax.ppermute(value, 'ell', [(e, e ^ 1) for e in range(32)])  5.47 us
    pallas_call x1, Pallas kernels, pixels(): pl.pallas_call(pixels_kernel, out_shape=(out, out), grid=(32 // SOURCES_S...  4.36 us
  transfers between devices with their start and end apart: 10, of which 1 were waited for; matrix products, arithmetic and copies ran while one was open for 0% of the time, Pallas kernels for 18%

profile of v5, /device:TPU:1, one launch (start us, length us, event | category | flops | bytes accessed | tf_op | source)
XLA Modules:
  0.0 115.1 jit_solution(1094814717467538134)
XLA Ops:
  0.6 0.0 copy-start
  0.7 0.7 copy-done
  1.3 0.1 dynamic-slice_bitcast_fusion.counts_ref
  1.4 0.0 copy-start.7
  1.4 1.0 copy-done.7
  2.5 0.9 radial_table.1
  3.4 3.8 %collective-permute-start.2 = (bf16[12,64,128]{2,1,0:T(8,128)(2,1)S(1)}, bf16[12,64,128]{2,1,0:T(8,128)(2,1)S(1)}, u32[]{:S(2)}, u32[]{:S(2)}) collective-permute-start(bf16[12,64,128]{2,1,0:T(8,128)(2,1)S(1)} %radial_table.1), channel_id=1, source_target_pairs={{0,32},{8,136},{16,48},{24,152},{32,0},{40,168},{48,16},{56,184},{... | collective-permute-start | bytes 589832 | tf_op jit(solution)/shard_map/ppermute | solution.py:507
  7.2 0.8 collective-permute-start.1
  8.0 0.7 collective-permute-start
  8.7 0.0 copy-start.1
  8.7 1.7 %copy-done.1 = bf16[32,24,1537]{2,1,0:T(8,128)(2,1)S(1)} copy-done((bf16[32,24,1537]{2,1,0:T(8,128)(2,1)S(1)}, bf16[32,24,1537]{2,1,0:T(8,128)(2,1)}, u32[]{:S(2)}) %copy-start.1) | copy-done | bytes 2360856
  10.4 5.3 %angular_blocks.3.refs_8_ = bf16[24,128,256]{2,1,0:T(8,128)(2,1)S(1)} custom-call(s32[1]{0:T(128)} %bitcast.e_ref, bf16[32,24,1537]{2,1,0:T(8,128)(2,1)S(1)} %copy-done.1, bf16[32,24,1537]{2,1,0:T(8,128)(2,1)S(1)} %copy-done.1), custom_call_target="tpu_custom_call" | custom-call | tf_op jit(solution)/shard_map/angular_blocks/pallas_call | solution.py:181
  15.7 0.0 copy-start.4
  15.7 1.2 %copy-done.4 = bf16[24,128,256]{2,1,0:T(8,128)(2,1)} copy-done((bf16[24,128,256]{2,1,0:T(8,128)(2,1)}, bf16[24,128,256]{2,1,0:T(8,128)(2,1)S(1)}, u32[]{:S(2)}) %copy-start.4) | copy-done | bytes 1572888
  16.9 0.0 copy-start.3
  16.9 0.0 collective-permute-done.2
  16.9 0.0 collective-permute-done.1
  16.9 0.0 collective-permute-done
  16.9 0.1 pad_maximum_fusion.refs_0_
  17.0 0.0 copy-start.8
  17.0 2.8 %collective-permute-start.5 = (bf16[48,64,128]{2,1,0:T(8,128)(2,1)S(1)}, bf16[48,64,128]{2,1,0:T(8,128)(2,1)S(1)}, u32[]{:S(2)}, u32[]{:S(2)}) collective-permute-start(bf16[48,64,128]{2,1,0:T(8,128)(2,1)S(1)} %pad_maximum_fusion.refs_0_), channel_id=1, source_target_pairs={{0,128},{8,40},{16,144},{24,56},{32,160},{40,8},{48,176},{56,24},{... | collective-permute-start | bytes 2359304 | tf_op jit(solution)/shard_map/ppermute | solution.py:507
  19.8 0.8 collective-permute-start.4
  20.7 0.6 collective-permute-start.3
  21.3 2.6 %angular_blocks.4.refs_9_ = bf16[24,128,128]{2,1,0:T(8,128)(2,1)S(1)} custom-call(s32[1]{0:T(128)} %bitcast.e_ref, bf16[32,24,1537]{2,1,0:T(8,128)(2,1)S(1)} %copy-done.1, bf16[32,24,1537]{2,1,0:T(8,128)(2,1)S(1)} %copy-done.1), custom_call_target="tpu_custom_call" | custom-call | tf_op jit(solution)/shard_map/angular_blocks/pallas_call | solution.py:181
  23.9 0.0 copy-start.5
  23.9 0.0 copy-start.2
  23.9 2.4 %collective-permute-start.6 = (bf16[48,64,128]{2,1,0:T(8,128)(2,1)S(1)}, bf16[48,64,128]{2,1,0:T(8,128)(2,1)S(1)}, u32[]{:S(2)}, u32[]{:S(2)}) collective-permute-start(bf16[48,64,128]{2,1,0:T(8,128)(2,1)S(1)} %pad_maximum_fusion.refs_0_), channel_id=1, source_target_pairs={{0,8},{8,0},{16,24},{24,16},{32,40},{40,32},{48,56},{56,48},{64,72... | collective-permute-start | bytes 2359304 | tf_op jit(solution)/shard_map/ppermute | solution.py:511
  26.4 0.0 copy-done.3
  26.4 10.3 %coeff_blocks.1.coeff_ref = bf16[14,32,48,128]{3,2,1,0:T(8,128)(2,1)} custom-call(s32[1]{0:T(128)} %bitcast.e_ref, bf16[2,32,24,1537]{3,2,1,0:T(8,128)(2,1)S(1)} %copy-done.3, bf16[2,32,24,1537]{3,2,1,0:T(8,128)(2,1)S(1)} %copy-done.3), custom_call_target="tpu_custom_call" | custom-call | tf_op jit(solution)/shard_map/coeff_blocks/pallas_call | solution.py:99
  36.7 0.0 copy-done.8
  36.7 0.0 copy-done.5
  36.7 0.0 collective-permute-done.5.refs_3_
  36.7 0.0 copy-start.9
  36.7 1.6 %collective-permute-done.4.refs_2_ = bf16[48,64,128]{2,1,0:T(8,128)(2,1)S(1)} collective-permute-done((bf16[48,64,128]{2,1,0:T(8,128)(2,1)S(1)}, bf16[48,64,128]{2,1,0:T(8,128)(2,1)S(1)}, u32[]{:S(2)}, u32[]{:S(2)}) %collective-permute-start.4) | collective-permute-done | bytes 786464 | tf_op jit(solution)/shard_map/ppermute | solution.py:507
  38.3 0.0 copy-start.10
  38.3 0.0 collective-permute-done.3.refs_1_
  38.3 0.0 copy-start.11
  38.3 2.5 %collective-permute-start.7 = (bf16[48,64,128]{2,1,0:T(8,128)(2,1)S(1)}, bf16[48,64,128]{2,1,0:T(8,128)(2,1)S(1)}, u32[]{:S(2)}, u32[]{:S(2)}) collective-permute-start(bf16[48,64,128]{2,1,0:T(8,128)(2,1)S(1)} %collective-permute-done.3.refs_1_), channel_id=1, source_target_pairs={{0,8},{8,0},{16,24},{24,16},{32,40},{40,32},{48,56},{56,48},{64,72... | collective-permute-start | bytes 2359304 | tf_op jit(solution)/shard_map/ppermute | solution.py:511
  40.8 0.1 collective-permute-start.8
  40.9 0.4 collective-permute-start.9
  41.3 0.0 copy-done.2
  41.3 2.1 %angular_blocks.5.refs_10_ = bf16[24,128,128]{2,1,0:T(8,128)(2,1)S(1)} custom-call(s32[1]{0:T(128)} %bitcast.e_ref, bf16[32,24,1537]{2,1,0:T(8,128)(2,1)S(1)} %copy-done.2, bf16[32,24,1537]{2,1,0:T(8,128)(2,1)S(1)} %copy-done.2), custom_call_target="tpu_custom_call" | custom-call | tf_op jit(solution)/shard_map/angular_blocks/pallas_call | solution.py:181
  43.4 0.0 copy-start.6
  43.4 0.9 copy-done.6
  44.3 0.0 collective-permute-done.6.refs_4_
  44.3 0.0 copy-start.12
  44.3 0.0 collective-permute-done.7.refs_5_
  44.3 0.0 copy-start.13
  44.4 0.0 collective-permute-done.8.refs_6_
  44.4 0.9 copy-done.12
  45.2 0.0 copy-start.14
  45.2 0.0 collective-permute-done.9.refs_7_
  45.2 0.0 copy-done.9
  45.2 0.0 copy-done.10
  45.2 0.0 copy-done.11
  45.3 0.2 copy-done.13
  45.5 0.6 copy-done.14
  46.1 0.0 copy-start.15
  46.1 0.9 copy-done.15
  47.1 25.4 %cycle_sums.1 = bf16[8,32,4,384]{3,2,1,0:T(4,128)(2,1)} custom-call(s32[1]{0:T(128)} %bitcast.e_ref, f32[96,48]{1,0:T(8,128)} %constant.19.clone.twist_ref, bf16[14,32,48,128]{3,2,1,0:T(8,128)(2,1)} %coeff_blocks.1.coeff_ref, bf16[48,64,128]{2,1,0:T(8,128)(2,1)} %copy-done.8, bf16[48,64,128]{2,1,0:T(8,128)(2,1)} %copy-done.11, ...), custom_call_target="tpu_custom_call" | custom-call | tf_op jit(solution)/shard_map/cycle_sums/pallas_call | solution.py:344
  72.5 38.3 %all_to_all.5 = bf16[256,4,384]{2,1,0:T(4,128)(2,1)S(1)} all-to-all(bf16[256,4,384]{2,1,0:T(4,128)(2,1)} %bitcast.7), channel_id=1, replica_groups=mesh['ell'=32,'rad'=8] {'rad','ell'}, dimensions={0} | all-to-all | bytes 1572864 | tf_op jit(solution)/shard_map/all_to_all | solution.py:544
  110.8 4.4 %pixels.1 = (f32[4,2,2048]{2,1,0:T(2,128)}, f32[4,2,2048]{2,1,0:T(2,128)}) custom-call(bf16[8,32,4,384]{3,2,1,0:T(4,128)(2,1)S(1)} %bitcast.6, bf16[32,96,1024]{2,1,0:T(8,128)(2,1)} %constant.20.clone.basis_ref), custom_call_target="tpu_custom_call" | custom-call | tf_op jit(solution)/shard_map/pixels/pallas_call | solution.py:433
Async XLA Ops:
  0.6 0.7 copy-start
  1.4 1.0 copy-start.7
  3.4 13.5 %collective-permute-start.2 = (bf16[12,64,128]{2,1,0:T(8,128)(2,1)S(1)}, bf16[12,64,128]{2,1,0:T(8,128)(2,1)S(1)}, u32[]{:S(2)}, u32[]{:S(2)}) collective-permute-start(bf16[12,64,128]{2,1,0:T(8,128)(2,1)S(1)} %radial_table.1), channel_id=1, source_target_pairs={{0,32},{8,136},{16,48},{24,152},{32,0},{40,168},{48,16},{56,184},{... | collective-permute-start | bytes 589832 | tf_op jit(solution)/shard_map/ppermute | solution.py:507
  7.2 9.6 %collective-permute-start.1 = (bf16[12,64,128]{2,1,0:T(8,128)(2,1)S(1)}, bf16[12,64,128]{2,1,0:T(8,128)(2,1)S(1)}, u32[]{:S(2)}, u32[]{:S(2)}) collective-permute-start(bf16[12,64,128]{2,1,0:T(8,128)(2,1)S(1)} %radial_table.1), channel_id=1, source_target_pairs={{0,48},{8,200},{16,0},{24,216},{32,16},{40,232},{48,32},{56,248},{... | collective-permute-start | bytes 589832 | tf_op jit(solution)/shard_map/ppermute | solution.py:507
  8.0 8.9 %collective-permute-start = (bf16[12,64,128]{2,1,0:T(8,128)(2,1)S(1)}, bf16[12,64,128]{2,1,0:T(8,128)(2,1)S(1)}, u32[]{:S(2)}, u32[]{:S(2)}) collective-permute-start(bf16[12,64,128]{2,1,0:T(8,128)(2,1)S(1)} %radial_table.1), channel_id=1, source_target_pairs={{0,16},{8,72},{16,32},{24,88},{32,48},{40,104},{48,0},{56,120},{64... | collective-permute-start | bytes 589832 | tf_op jit(solution)/shard_map/ppermute | solution.py:507
  8.7 1.7 %copy-start.1 = (bf16[32,24,1537]{2,1,0:T(8,128)(2,1)S(1)}, bf16[32,24,1537]{2,1,0:T(8,128)(2,1)}, u32[]{:S(2)}) copy-start(bf16[32,24,1537]{2,1,0:T(8,128)(2,1)} %second_ref.7) | copy-start | bytes 7082500
  15.7 1.2 %copy-start.4 = (bf16[24,128,256]{2,1,0:T(8,128)(2,1)}, bf16[24,128,256]{2,1,0:T(8,128)(2,1)S(1)}, u32[]{:S(2)}) copy-start(bf16[24,128,256]{2,1,0:T(8,128)(2,1)S(1)} %angular_blocks.3.refs_8_) | copy-start | bytes 4718596
  16.9 9.5 %copy-start.3 = (bf16[2,32,24,1537]{3,2,1,0:T(8,128)(2,1)S(1)}, bf16[2,32,24,1537]{3,2,1,0:T(8,128)(2,1)}, u32[]{:S(2)}) copy-start(bf16[2,32,24,1537]{3,2,1,0:T(8,128)(2,1)} %second_ref.5) | copy-start | bytes 14164996
  17.0 19.7 %copy-start.8 = (bf16[48,64,128]{2,1,0:T(8,128)(2,1)}, bf16[48,64,128]{2,1,0:T(8,128)(2,1)S(1)}, u32[]{:S(2)}) copy-start(bf16[48,64,128]{2,1,0:T(8,128)(2,1)S(1)} %pad_maximum_fusion.refs_0_) | copy-start | bytes 2359300
  17.0 19.7 %collective-permute-start.5 = (bf16[48,64,128]{2,1,0:T(8,128)(2,1)S(1)}, bf16[48,64,128]{2,1,0:T(8,128)(2,1)S(1)}, u32[]{:S(2)}, u32[]{:S(2)}) collective-permute-start(bf16[48,64,128]{2,1,0:T(8,128)(2,1)S(1)} %pad_maximum_fusion.refs_0_), channel_id=1, source_target_pairs={{0,128},{8,40},{16,144},{24,56},{32,160},{40,8},{48,176},{56,24},{... | collective-permute-start | bytes 2359304 | tf_op jit(solution)/shard_map/ppermute | solution.py:507
  19.8 18.4 %collective-permute-start.4 = (bf16[48,64,128]{2,1,0:T(8,128)(2,1)S(1)}, bf16[48,64,128]{2,1,0:T(8,128)(2,1)S(1)}, u32[]{:S(2)}, u32[]{:S(2)}) collective-permute-start(bf16[48,64,128]{2,1,0:T(8,128)(2,1)S(1)} %pad_maximum_fusion.refs_0_), channel_id=1, source_target_pairs={{0,192},{8,56},{16,208},{24,8},{32,224},{40,24},{48,240},{56,40},{... | collective-permute-start | bytes 2359304 | tf_op jit(solution)/shard_map/ppermute | solution.py:507
  20.7 17.6 %collective-permute-start.3 = (bf16[48,64,128]{2,1,0:T(8,128)(2,1)S(1)}, bf16[48,64,128]{2,1,0:T(8,128)(2,1)S(1)}, u32[]{:S(2)}, u32[]{:S(2)}) collective-permute-start(bf16[48,64,128]{2,1,0:T(8,128)(2,1)S(1)} %pad_maximum_fusion.refs_0_), channel_id=1, source_target_pairs={{0,64},{8,24},{16,80},{24,40},{32,96},{40,56},{48,112},{56,8},{64,... | collective-permute-start | bytes 2359304 | tf_op jit(solution)/shard_map/ppermute | solution.py:507
  23.9 12.8 %copy-start.5 = (bf16[24,128,128]{2,1,0:T(8,128)(2,1)}, bf16[24,128,128]{2,1,0:T(8,128)(2,1)S(1)}, u32[]{:S(2)}) copy-start(bf16[24,128,128]{2,1,0:T(8,128)(2,1)S(1)} %angular_blocks.4.refs_9_) | copy-start | bytes 2359300
  23.9 17.4 %copy-start.2 = (bf16[32,24,1537]{2,1,0:T(8,128)(2,1)S(1)}, bf16[32,24,1537]{2,1,0:T(8,128)(2,1)}, u32[]{:S(2)}) copy-start(bf16[32,24,1537]{2,1,0:T(8,128)(2,1)} %second_ref.7) | copy-start | bytes 7082500
  23.9 20.4 %collective-permute-start.6 = (bf16[48,64,128]{2,1,0:T(8,128)(2,1)S(1)}, bf16[48,64,128]{2,1,0:T(8,128)(2,1)S(1)}, u32[]{:S(2)}, u32[]{:S(2)}) collective-permute-start(bf16[48,64,128]{2,1,0:T(8,128)(2,1)S(1)} %pad_maximum_fusion.refs_0_), channel_id=1, source_target_pairs={{0,8},{8,0},{16,24},{24,16},{32,40},{40,32},{48,56},{56,48},{64,72... | collective-permute-start | bytes 2359304 | tf_op jit(solution)/shard_map/ppermute | solution.py:511
  36.7 8.5 %copy-start.9 = (bf16[48,64,128]{2,1,0:T(8,128)(2,1)}, bf16[48,64,128]{2,1,0:T(8,128)(2,1)S(1)}, u32[]{:S(2)}) copy-start(bf16[48,64,128]{2,1,0:T(8,128)(2,1)S(1)} %collective-permute-done.5.refs_3_) | copy-start | bytes 2359300
  38.3 6.9 %copy-start.10 = (bf16[48,64,128]{2,1,0:T(8,128)(2,1)}, bf16[48,64,128]{2,1,0:T(8,128)(2,1)S(1)}, u32[]{:S(2)}) copy-start(bf16[48,64,128]{2,1,0:T(8,128)(2,1)S(1)} %collective-permute-done.4.refs_2_) | copy-start | bytes 2359300
  38.3 6.9 %copy-start.11 = (bf16[48,64,128]{2,1,0:T(8,128)(2,1)}, bf16[48,64,128]{2,1,0:T(8,128)(2,1)S(1)}, u32[]{:S(2)}) copy-start(bf16[48,64,128]{2,1,0:T(8,128)(2,1)S(1)} %collective-permute-done.3.refs_1_) | copy-start | bytes 2359300
  38.3 6.0 %collective-permute-start.7 = (bf16[48,64,128]{2,1,0:T(8,128)(2,1)S(1)}, bf16[48,64,128]{2,1,0:T(8,128)(2,1)S(1)}, u32[]{:S(2)}, u32[]{:S(2)}) collective-permute-start(bf16[48,64,128]{2,1,0:T(8,128)(2,1)S(1)} %collective-permute-done.3.refs_1_), channel_id=1, source_target_pairs={{0,8},{8,0},{16,24},{24,16},{32,40},{40,32},{48,56},{56,48},{64,72... | collective-permute-start | bytes 2359304 | tf_op jit(solution)/shard_map/ppermute | solution.py:511
  40.8 3.5 %collective-permute-start.8 = (bf16[48,64,128]{2,1,0:T(8,128)(2,1)S(1)}, bf16[48,64,128]{2,1,0:T(8,128)(2,1)S(1)}, u32[]{:S(2)}, u32[]{:S(2)}) collective-permute-start(bf16[48,64,128]{2,1,0:T(8,128)(2,1)S(1)} %collective-permute-done.4.refs_2_), channel_id=1, source_target_pairs={{0,8},{8,0},{16,24},{24,16},{32,40},{40,32},{48,56},{56,48},{64,72... | collective-permute-start | bytes 2359304 | tf_op jit(solution)/shard_map/ppermute | solution.py:511
  40.9 4.3 %collective-permute-start.9 = (bf16[48,64,128]{2,1,0:T(8,128)(2,1)S(1)}, bf16[48,64,128]{2,1,0:T(8,128)(2,1)S(1)}, u32[]{:S(2)}, u32[]{:S(2)}) collective-permute-start(bf16[48,64,128]{2,1,0:T(8,128)(2,1)S(1)} %collective-permute-done.5.refs_3_), channel_id=1, source_target_pairs={{0,8},{8,0},{16,24},{24,16},{32,40},{40,32},{48,56},{56,48},{64,72... | collective-permute-start | bytes 2359304 | tf_op jit(solution)/shard_map/ppermute | solution.py:511
  43.4 0.9 copy-start.6
  44.3 0.9 copy-start.12
  44.3 1.1 copy-start.13
  45.2 0.9 copy-start.14
  46.1 0.9 copy-start.15

commit v6 on v5

--- a/solution.py
+++ b/solution.py
@@ -19,7 +19,7 @@
 PITCH = SPAN + 8
 KPAD = 512
 ROW_PITCH = 40
-PIECE = 12
+PIECE = 6
 SHIFTS = (0, 1, -1, 2)
 ANGULAR_PARTS = ((0, 2), (2, 1), (3, 1))
 BF = jnp.bfloat16
@@ -228,7 +228,7 @@
     for part, (first_quad, quads) in enumerate(ANGULAR_PARTS):
         place = angular_ref.at[:, :, pl.ds(128 * first_quad, 128 * quads)]
         fetches.append(pltpu.make_async_copy(angular[part], place, angular_sems.at[part]))
-    first_piece = p0 // 4 // PIECE
+    first_piece = p0 // 8 // PIECE
 
     @pl.when(k == 0)
     def _():
@@ -250,9 +250,9 @@
 
     last_group = L // 4 - 1
     wait_from = jnp.where(
-        k == 0, first_piece, jnp.minimum(p0 // 4 + GROUPS * k - 1, last_group) // PIECE + 1
+        k == 0, first_piece, jnp.minimum(p0 // 4 + GROUPS * k - 1, last_group) // (2 * PIECE) + 1
     )
-    wait_to = jnp.minimum(p0 // 4 + GROUPS * k + GROUPS - 1, last_group) // PIECE + 1
+    wait_to = jnp.minimum(p0 // 4 + GROUPS * k + GROUPS - 1, last_group) // (2 * PIECE) + 1
 
     def arrive(piece, carry):
         pltpu.make_async_copy(
@@ -262,24 +262,29 @@
 
     lax.fori_loop(wait_from, wait_to, arrive, 0)
 
-    lane = lax.broadcasted_iota(jnp.int32, (64, 128), 1)
-    slots = [(lane & 3) == j for j in range(4)]
-
-    def group(g, carry):
-        table = table_ref[jnp.minimum(base + g, last_group)]
-        weights = jnp.concatenate(
-            [jnp.where(slots[j], table, jnp.zeros_like(table)) for j in range(4)], axis=0
-        )
-        radial = lax.dot_general(
-            coeff_ref[0, g], weights, (((1,), (1,)), ((), ())), preferred_element_type=F32
-        )
-        radial = radial.astype(BF).astype(F32)
-        at = k * GROUPS + g
-        left[pl.ds(at, 48, stride=PITCH), :] = radial[:, :128]
-        right[pl.ds(at, 48, stride=PITCH), :] = radial[:, 128:]
+    near_lane = lax.broadcasted_iota(jnp.int32, (128, 128), 1) < 64
+    slot_row = lax.broadcasted_iota(jnp.int32, (128, 128), 0) & 3
+    left_slots = slot_row == jnp.where(near_lane, 0, 1)
+    right_slots = slot_row == jnp.where(near_lane, 2, 3)
+
+    def group_pair(g, carry):
+        table = table_ref[jnp.minimum(base // 2 + g, L // 8 - 1)]
+        turned_table = pltpu.roll(table, 64, 1)
+        zero = jnp.zeros_like(table)
+        for half in range(2):
+            one, two = (table, turned_table) if half == 0 else (turned_table, table)
+            doubled = jnp.where(near_lane, one, two)
+            weights = jnp.concatenate(
+                [jnp.where(left_slots, doubled, zero), jnp.where(right_slots, doubled, zero)], axis=1
+            )
+            radial = jnp.dot(coeff_ref[0, 2 * g + half], weights, preferred_element_type=F32)
+            radial = radial.astype(BF).astype(F32)
+            at = k * GROUPS + 2 * g + half
+            left[pl.ds(at, 48, stride=PITCH), :] = radial[:, :128]
+            right[pl.ds(at, 48, stride=PITCH), :] = radial[:, 128:]
         return carry
 
-    lax.fori_loop(0, GROUPS, group, 0, unroll=True)
+    lax.fori_loop(0, GROUPS // 2, group_pair, 0, unroll=True)
 
     @pl.when(k == STEPS - 1)
     def _():
@@ -356,7 +361,7 @@
                 pltpu.VMEM((48 * PITCH, 128), F32),
                 pltpu.VMEM((48 * PITCH, 128), F32),
                 pltpu.VMEM((32 * 96, 128), F32),
-                pltpu.VMEM((L // 4, 64, 128), BF),
+                pltpu.VMEM((L // 8, 128, 128), BF),
                 pltpu.VMEM((PAIR_DEV, 128, KPAD), BF),
                 pltpu.SemaphoreType.DMA((32,)),
                 pltpu.SemaphoreType.DMA((3,)),
@@ -467,8 +472,9 @@
         return carry
 
     lax.fori_loop(0, 8, one, 0, unroll=2)
-    for g in range(width // 4):
-        out_ref[g] = grouped[g].astype(BF)
+    for g in range(width // 8):
+        turned = [jnp.transpose(grouped[2 * g + d]) for d in range(2)]
+        out_ref[g] = jnp.concatenate(turned, axis=1).astype(BF)
 
 
 def radial_table(bessel, mode_counts):
@@ -476,7 +482,7 @@
     counts = lax.dynamic_slice_in_dim(mode_counts, lax.axis_index("ell") * width, width)
     return pl.pallas_call(
         table_kernel,
-        out_shape=jax.ShapeDtypeStruct((width // 4, 64, 128), BF),
+        out_shape=jax.ShapeDtypeStruct((width // 8, 128, 128), BF),
         grid_spec=pltpu.PrefetchScalarGridSpec(
             num_scalar_prefetch=1,
             grid=(1,),
@@ -484,7 +490,7 @@
                 pl.BlockSpec(bessel.shape, lambda k, s: (0, 0, 0, 0)),
                 pl.BlockSpec((1, width), lambda k, s: (0, 0)),
             ],
-            out_specs=pl.BlockSpec((width // 4, 64, 128), lambda k, s: (0, 0, 0)),
+            out_specs=pl.BlockSpec((width // 8, 128, 128), lambda k, s: (0, 0, 0)),
             scratch_shapes=[
                 pltpu.VMEM((64 * ROW_PITCH, 128), F32),
                 pltpu.VMEM((width // 4, 64, 128), F32),

time: 116 us -> 114 us (0.983)
  Pallas kernels: 51 us -> 49.7 us
    pallas_call x1, Pallas kernels: 25.4 us -> 23.8 us  [cycle_sums(): pl.pallas_call(sums_kernel, out_shape=jax.ShapeDtypeStruct((8, 32, 4, 384...]
where the time goes in v6:
time: 114 us
  Pallas kernels  49.7 us (44%)
  blocking collectives  38.3 us (34%)
  starting transfers between devices  15.1 us (13%)
  local copies, waits for them, and re-layouts  8.29 us (7%)
  waiting for transfers between devices  1.59 us (1%)
    all_to_all x1, blocking collectives, local(): lax.all_to_all(sums.reshape(256, 4, 384), ('rad', 'ell'), split_axis=0, c...  38.3 us
    pallas_call x1, Pallas kernels, cycle_sums(): pl.pallas_call(sums_kernel, out_shape=jax.ShapeDtypeStruct((8, 32, 4, 384...  23.8 us
    pallas_call x1, Pallas kernels, coeff_blocks(): pl.pallas_call(coeff_kernel, out_shape=jax.ShapeDtypeStruct((STEPS, GROUP...  10.3 us
    pallas_call x3, Pallas kernels, angular_blocks(): pl.pallas_call(functools.partial(angular_kernel, start), out_shape=jax.Sh...  9.94 us
    ppermute x6, starting transfers between devices, ring_shift(): return lax.ppermute(value, 'ell', pairs)  9.59 us
    unnamed x32, local copies, waits for them, and re-layouts  8.21 us
    ppermute x4, starting transfers between devices, other_core(): return lax.ppermute(value, 'ell', [(e, e ^ 1) for e in range(32)])  5.49 us
    pallas_call x1, Pallas kernels, pixels(): pl.pallas_call(pixels_kernel, out_shape=(out, out), grid=(32 // SOURCES_S...  4.36 us
  transfers between devices with their start and end apart: 10, of which 1 were waited for; matrix products, arithmetic and copies ran while one was open for 0% of the time, Pallas kernels for 18%

profile of v6, /device:TPU:1, one launch (start us, length us, event | category | flops | bytes accessed | tf_op | source)
XLA Modules:
  0.0 113.9 jit_solution(15076970016426211665)
XLA Ops:
  0.6 0.0 copy-start
  0.7 0.7 copy-done
  1.3 0.1 dynamic-slice_bitcast_fusion.counts_ref
  1.4 0.0 copy-start.7
  1.4 1.0 copy-done.7
  2.5 1.3 %radial_table.1 = bf16[6,128,128]{2,1,0:T(8,128)(2,1)S(1)} custom-call(s32[1]{0:T(128)} %bitcast.1.r_ref, bf16[2,32,32,48]{3,2,1,0:T(8,128)(2,1)S(1)} %copy-done.7, s32[1,48]{1,0:T(1,128)S(1)} %dynamic-slice_bitcast_fusion.counts_ref), custom_call_target="tpu_custom_call" | custom-call | tf_op jit(solution)/shard_map/radial_table/pallas_call | solution.py:483
  3.7 3.8 %collective-permute-start.2 = (bf16[6,128,128]{2,1,0:T(8,128)(2,1)S(1)}, bf16[6,128,128]{2,1,0:T(8,128)(2,1)S(1)}, u32[]{:S(2)}, u32[]{:S(2)}) collective-permute-start(bf16[6,128,128]{2,1,0:T(8,128)(2,1)S(1)} %radial_table.1), channel_id=1, source_target_pairs={{0,32},{8,136},{16,48},{24,152},{32,0},{40,168},{48,16},{56,184},{... | collective-permute-start | bytes 589832 | tf_op jit(solution)/shard_map/ppermute | solution.py:513
  7.5 0.8 collective-permute-start.1
  8.3 0.7 collective-permute-start
  9.0 0.0 copy-start.1
  9.0 1.7 %copy-done.1 = bf16[32,24,1537]{2,1,0:T(8,128)(2,1)S(1)} copy-done((bf16[32,24,1537]{2,1,0:T(8,128)(2,1)S(1)}, bf16[32,24,1537]{2,1,0:T(8,128)(2,1)}, u32[]{:S(2)}) %copy-start.1) | copy-done | bytes 2360856
  10.7 5.3 %angular_blocks.3.refs_8_ = bf16[24,128,256]{2,1,0:T(8,128)(2,1)S(1)} custom-call(s32[1]{0:T(128)} %bitcast.e_ref, bf16[32,24,1537]{2,1,0:T(8,128)(2,1)S(1)} %copy-done.1, bf16[32,24,1537]{2,1,0:T(8,128)(2,1)S(1)} %copy-done.1), custom_call_target="tpu_custom_call" | custom-call | tf_op jit(solution)/shard_map/angular_blocks/pallas_call | solution.py:181
  16.0 0.0 copy-start.4
  16.0 1.2 %copy-done.4 = bf16[24,128,256]{2,1,0:T(8,128)(2,1)} copy-done((bf16[24,128,256]{2,1,0:T(8,128)(2,1)}, bf16[24,128,256]{2,1,0:T(8,128)(2,1)S(1)}, u32[]{:S(2)}) %copy-start.4) | copy-done | bytes 1572888
  17.2 0.0 copy-start.3
  17.2 0.0 collective-permute-done.2
  17.2 0.0 collective-permute-done.1
  17.2 0.0 collective-permute-done
  17.2 0.1 pad_maximum_fusion.refs_0_
  17.3 0.0 copy-start.8
  17.3 2.8 %collective-permute-start.5 = (bf16[24,128,128]{2,1,0:T(8,128)(2,1)S(1)}, bf16[24,128,128]{2,1,0:T(8,128)(2,1)S(1)}, u32[]{:S(2)}, u32[]{:S(2)}) collective-permute-start(bf16[24,128,128]{2,1,0:T(8,128)(2,1)S(1)} %pad_maximum_fusion.refs_0_), channel_id=1, source_target_pairs={{0,128},{8,40},{16,144},{24,56},{32,160},{40,8},{48,176},{56,24},{... | collective-permute-start | bytes 2359304 | tf_op jit(solution)/shard_map/ppermute | solution.py:513
  20.1 0.9 collective-permute-start.4
  21.0 0.6 collective-permute-start.3
  21.6 2.6 %angular_blocks.4.refs_9_ = bf16[24,128,128]{2,1,0:T(8,128)(2,1)S(1)} custom-call(s32[1]{0:T(128)} %bitcast.e_ref, bf16[32,24,1537]{2,1,0:T(8,128)(2,1)S(1)} %copy-done.1, bf16[32,24,1537]{2,1,0:T(8,128)(2,1)S(1)} %copy-done.1), custom_call_target="tpu_custom_call" | custom-call | tf_op jit(solution)/shard_map/angular_blocks/pallas_call | solution.py:181
  24.2 0.0 copy-start.5
  24.2 0.0 copy-start.2
  24.2 2.4 %collective-permute-start.6 = (bf16[24,128,128]{2,1,0:T(8,128)(2,1)S(1)}, bf16[24,128,128]{2,1,0:T(8,128)(2,1)S(1)}, u32[]{:S(2)}, u32[]{:S(2)}) collective-permute-start(bf16[24,128,128]{2,1,0:T(8,128)(2,1)S(1)} %pad_maximum_fusion.refs_0_), channel_id=1, source_target_pairs={{0,8},{8,0},{16,24},{24,16},{32,40},{40,32},{48,56},{56,48},{64,72... | collective-permute-start | bytes 2359304 | tf_op jit(solution)/shard_map/ppermute | solution.py:517
  26.7 0.0 copy-done.3
  26.7 10.3 %coeff_blocks.1.coeff_ref = bf16[14,32,48,128]{3,2,1,0:T(8,128)(2,1)} custom-call(s32[1]{0:T(128)} %bitcast.e_ref, bf16[2,32,24,1537]{3,2,1,0:T(8,128)(2,1)S(1)} %copy-done.3, bf16[2,32,24,1537]{3,2,1,0:T(8,128)(2,1)S(1)} %copy-done.3), custom_call_target="tpu_custom_call" | custom-call | tf_op jit(solution)/shard_map/coeff_blocks/pallas_call | solution.py:99
  37.0 0.0 copy-done.8
  37.0 0.0 copy-done.5
  37.0 0.0 collective-permute-done.5.refs_3_
  37.0 0.0 copy-start.9
  37.0 1.6 %collective-permute-done.4.refs_2_ = bf16[24,128,128]{2,1,0:T(8,128)(2,1)S(1)} collective-permute-done((bf16[24,128,128]{2,1,0:T(8,128)(2,1)S(1)}, bf16[24,128,128]{2,1,0:T(8,128)(2,1)S(1)}, u32[]{:S(2)}, u32[]{:S(2)}) %collective-permute-start.4) | collective-permute-done | bytes 786464 | tf_op jit(solution)/shard_map/ppermute | solution.py:513
  38.6 0.0 copy-start.10
  38.6 0.0 collective-permute-done.3.refs_1_
  38.6 0.0 copy-start.11
  38.6 2.5 %collective-permute-start.7 = (bf16[24,128,128]{2,1,0:T(8,128)(2,1)S(1)}, bf16[24,128,128]{2,1,0:T(8,128)(2,1)S(1)}, u32[]{:S(2)}, u32[]{:S(2)}) collective-permute-start(bf16[24,128,128]{2,1,0:T(8,128)(2,1)S(1)} %collective-permute-done.3.refs_1_), channel_id=1, source_target_pairs={{0,8},{8,0},{16,24},{24,16},{32,40},{40,32},{48,56},{56,48},{64,72... | collective-permute-start | bytes 2359304 | tf_op jit(solution)/shard_map/ppermute | solution.py:517
  41.1 0.1 collective-permute-start.8
  41.2 0.4 collective-permute-start.9
  41.7 0.0 copy-done.2
  41.7 2.1 %angular_blocks.5.refs_10_ = bf16[24,128,128]{2,1,0:T(8,128)(2,1)S(1)} custom-call(s32[1]{0:T(128)} %bitcast.e_ref, bf16[32,24,1537]{2,1,0:T(8,128)(2,1)S(1)} %copy-done.2, bf16[32,24,1537]{2,1,0:T(8,128)(2,1)S(1)} %copy-done.2), custom_call_target="tpu_custom_call" | custom-call | tf_op jit(solution)/shard_map/angular_blocks/pallas_call | solution.py:181
  43.7 0.0 copy-start.6
  43.8 0.9 copy-done.6
  44.6 0.0 collective-permute-done.6.refs_4_
  44.7 0.0 copy-start.12
  44.7 0.0 collective-permute-done.7.refs_5_
  44.7 0.0 copy-start.13
  44.7 0.0 collective-permute-done.8.refs_6_
  44.7 0.9 copy-done.12
  45.5 0.0 copy-start.14
  45.5 0.0 collective-permute-done.9.refs_7_
  45.5 0.0 copy-done.9
  45.5 0.0 copy-done.10
  45.5 0.0 copy-done.11
  45.6 0.2 copy-done.13
  45.8 0.6 copy-done.14
  46.4 0.0 copy-start.15
  46.4 0.9 copy-done.15
  47.4 23.8 %cycle_sums.1 = bf16[8,32,4,384]{3,2,1,0:T(4,128)(2,1)} custom-call(s32[1]{0:T(128)} %bitcast.e_ref, f32[96,48]{1,0:T(8,128)} %constant.19.clone.twist_ref, bf16[14,32,48,128]{3,2,1,0:T(8,128)(2,1)} %coeff_blocks.1.coeff_ref, bf16[24,128,128]{2,1,0:T(8,128)(2,1)} %copy-done.8, bf16[24,128,128]{2,1,0:T(8,128)(2,1)} %copy-done.11, ...), custom_call_target="tpu_custom_call" | custom-call | tf_op jit(solution)/shard_map/cycle_sums/pallas_call | solution.py:349
  71.2 38.3 %all_to_all.5 = bf16[256,4,384]{2,1,0:T(4,128)(2,1)S(1)} all-to-all(bf16[256,4,384]{2,1,0:T(4,128)(2,1)} %bitcast.7), channel_id=1, replica_groups=mesh['ell'=32,'rad'=8] {'rad','ell'}, dimensions={0} | all-to-all | bytes 1572864 | tf_op jit(solution)/shard_map/all_to_all | solution.py:550
  109.5 4.4 %pixels.1 = (f32[4,2,2048]{2,1,0:T(2,128)}, f32[4,2,2048]{2,1,0:T(2,128)}) custom-call(bf16[8,32,4,384]{3,2,1,0:T(4,128)(2,1)S(1)} %bitcast.6, bf16[32,96,1024]{2,1,0:T(8,128)(2,1)} %constant.20.clone.basis_ref), custom_call_target="tpu_custom_call" | custom-call | tf_op jit(solution)/shard_map/pixels/pallas_call | solution.py:438
Async XLA Ops:
  0.6 0.7 copy-start
  1.4 1.0 copy-start.7
  3.7 13.5 %collective-permute-start.2 = (bf16[6,128,128]{2,1,0:T(8,128)(2,1)S(1)}, bf16[6,128,128]{2,1,0:T(8,128)(2,1)S(1)}, u32[]{:S(2)}, u32[]{:S(2)}) collective-permute-start(bf16[6,128,128]{2,1,0:T(8,128)(2,1)S(1)} %radial_table.1), channel_id=1, source_target_pairs={{0,32},{8,136},{16,48},{24,152},{32,0},{40,168},{48,16},{56,184},{... | collective-permute-start | bytes 589832 | tf_op jit(solution)/shard_map/ppermute | solution.py:513
  7.5 9.6 %collective-permute-start.1 = (bf16[6,128,128]{2,1,0:T(8,128)(2,1)S(1)}, bf16[6,128,128]{2,1,0:T(8,128)(2,1)S(1)}, u32[]{:S(2)}, u32[]{:S(2)}) collective-permute-start(bf16[6,128,128]{2,1,0:T(8,128)(2,1)S(1)} %radial_table.1), channel_id=1, source_target_pairs={{0,48},{8,200},{16,0},{24,216},{32,16},{40,232},{48,32},{56,248},{... | collective-permute-start | bytes 589832 | tf_op jit(solution)/shard_map/ppermute | solution.py:513
  8.3 8.9 %collective-permute-start = (bf16[6,128,128]{2,1,0:T(8,128)(2,1)S(1)}, bf16[6,128,128]{2,1,0:T(8,128)(2,1)S(1)}, u32[]{:S(2)}, u32[]{:S(2)}) collective-permute-start(bf16[6,128,128]{2,1,0:T(8,128)(2,1)S(1)} %radial_table.1), channel_id=1, source_target_pairs={{0,16},{8,72},{16,32},{24,88},{32,48},{40,104},{48,0},{56,120},{64... | collective-permute-start | bytes 589832 | tf_op jit(solution)/shard_map/ppermute | solution.py:513
  9.0 1.7 %copy-start.1 = (bf16[32,24,1537]{2,1,0:T(8,128)(2,1)S(1)}, bf16[32,24,1537]{2,1,0:T(8,128)(2,1)}, u32[]{:S(2)}) copy-start(bf16[32,24,1537]{2,1,0:T(8,128)(2,1)} %second_ref.7) | copy-start | bytes 7082500
  16.0 1.2 %copy-start.4 = (bf16[24,128,256]{2,1,0:T(8,128)(2,1)}, bf16[24,128,256]{2,1,0:T(8,128)(2,1)S(1)}, u32[]{:S(2)}) copy-start(bf16[24,128,256]{2,1,0:T(8,128)(2,1)S(1)} %angular_blocks.3.refs_8_) | copy-start | bytes 4718596
  17.2 9.5 %copy-start.3 = (bf16[2,32,24,1537]{3,2,1,0:T(8,128)(2,1)S(1)}, bf16[2,32,24,1537]{3,2,1,0:T(8,128)(2,1)}, u32[]{:S(2)}) copy-start(bf16[2,32,24,1537]{3,2,1,0:T(8,128)(2,1)} %second_ref.5) | copy-start | bytes 14164996
  17.3 19.7 %copy-start.8 = (bf16[24,128,128]{2,1,0:T(8,128)(2,1)}, bf16[24,128,128]{2,1,0:T(8,128)(2,1)S(1)}, u32[]{:S(2)}) copy-start(bf16[24,128,128]{2,1,0:T(8,128)(2,1)S(1)} %pad_maximum_fusion.refs_0_) | copy-start | bytes 2359300
  17.3 19.7 %collective-permute-start.5 = (bf16[24,128,128]{2,1,0:T(8,128)(2,1)S(1)}, bf16[24,128,128]{2,1,0:T(8,128)(2,1)S(1)}, u32[]{:S(2)}, u32[]{:S(2)}) collective-permute-start(bf16[24,128,128]{2,1,0:T(8,128)(2,1)S(1)} %pad_maximum_fusion.refs_0_), channel_id=1, source_target_pairs={{0,128},{8,40},{16,144},{24,56},{32,160},{40,8},{48,176},{56,24},{... | collective-permute-start | bytes 2359304 | tf_op jit(solution)/shard_map/ppermute | solution.py:513
  20.1 18.5 %collective-permute-start.4 = (bf16[24,128,128]{2,1,0:T(8,128)(2,1)S(1)}, bf16[24,128,128]{2,1,0:T(8,128)(2,1)S(1)}, u32[]{:S(2)}, u32[]{:S(2)}) collective-permute-start(bf16[24,128,128]{2,1,0:T(8,128)(2,1)S(1)} %pad_maximum_fusion.refs_0_), channel_id=1, source_target_pairs={{0,192},{8,56},{16,208},{24,8},{32,224},{40,24},{48,240},{56,40},{... | collective-permute-start | bytes 2359304 | tf_op jit(solution)/shard_map/ppermute | solution.py:513
  21.0 17.6 %collective-permute-start.3 = (bf16[24,128,128]{2,1,0:T(8,128)(2,1)S(1)}, bf16[24,128,128]{2,1,0:T(8,128)(2,1)S(1)}, u32[]{:S(2)}, u32[]{:S(2)}) collective-permute-start(bf16[24,128,128]{2,1,0:T(8,128)(2,1)S(1)} %pad_maximum_fusion.refs_0_), channel_id=1, source_target_pairs={{0,64},{8,24},{16,80},{24,40},{32,96},{40,56},{48,112},{56,8},{64,... | collective-permute-start | bytes 2359304 | tf_op jit(solution)/shard_map/ppermute | solution.py:513
  24.2 12.8 %copy-start.5 = (bf16[24,128,128]{2,1,0:T(8,128)(2,1)}, bf16[24,128,128]{2,1,0:T(8,128)(2,1)S(1)}, u32[]{:S(2)}) copy-start(bf16[24,128,128]{2,1,0:T(8,128)(2,1)S(1)} %angular_blocks.4.refs_9_) | copy-start | bytes 2359300
  24.2 17.4 %copy-start.2 = (bf16[32,24,1537]{2,1,0:T(8,128)(2,1)S(1)}, bf16[32,24,1537]{2,1,0:T(8,128)(2,1)}, u32[]{:S(2)}) copy-start(bf16[32,24,1537]{2,1,0:T(8,128)(2,1)} %second_ref.7) | copy-start | bytes 7082500
  24.2 20.4 %collective-permute-start.6 = (bf16[24,128,128]{2,1,0:T(8,128)(2,1)S(1)}, bf16[24,128,128]{2,1,0:T(8,128)(2,1)S(1)}, u32[]{:S(2)}, u32[]{:S(2)}) collective-permute-start(bf16[24,128,128]{2,1,0:T(8,128)(2,1)S(1)} %pad_maximum_fusion.refs_0_), channel_id=1, source_target_pairs={{0,8},{8,0},{16,24},{24,16},{32,40},{40,32},{48,56},{56,48},{64,72... | collective-permute-start | bytes 2359304 | tf_op jit(solution)/shard_map/ppermute | solution.py:517
  37.0 8.5 %copy-start.9 = (bf16[24,128,128]{2,1,0:T(8,128)(2,1)}, bf16[24,128,128]{2,1,0:T(8,128)(2,1)S(1)}, u32[]{:S(2)}) copy-start(bf16[24,128,128]{2,1,0:T(8,128)(2,1)S(1)} %collective-permute-done.5.refs_3_) | copy-start | bytes 2359300
  38.6 6.9 %copy-start.10 = (bf16[24,128,128]{2,1,0:T(8,128)(2,1)}, bf16[24,128,128]{2,1,0:T(8,128)(2,1)S(1)}, u32[]{:S(2)}) copy-start(bf16[24,128,128]{2,1,0:T(8,128)(2,1)S(1)} %collective-permute-done.4.refs_2_) | copy-start | bytes 2359300
  38.6 6.9 %copy-start.11 = (bf16[24,128,128]{2,1,0:T(8,128)(2,1)}, bf16[24,128,128]{2,1,0:T(8,128)(2,1)S(1)}, u32[]{:S(2)}) copy-start(bf16[24,128,128]{2,1,0:T(8,128)(2,1)S(1)} %collective-permute-done.3.refs_1_) | copy-start | bytes 2359300
  38.6 6.0 %collective-permute-start.7 = (bf16[24,128,128]{2,1,0:T(8,128)(2,1)S(1)}, bf16[24,128,128]{2,1,0:T(8,128)(2,1)S(1)}, u32[]{:S(2)}, u32[]{:S(2)}) collective-permute-start(bf16[24,128,128]{2,1,0:T(8,128)(2,1)S(1)} %collective-permute-done.3.refs_1_), channel_id=1, source_target_pairs={{0,8},{8,0},{16,24},{24,16},{32,40},{40,32},{48,56},{56,48},{64,72... | collective-permute-start | bytes 2359304 | tf_op jit(solution)/shard_map/ppermute | solution.py:517
  41.1 3.5 %collective-permute-start.8 = (bf16[24,128,128]{2,1,0:T(8,128)(2,1)S(1)}, bf16[24,128,128]{2,1,0:T(8,128)(2,1)S(1)}, u32[]{:S(2)}, u32[]{:S(2)}) collective-permute-start(bf16[24,128,128]{2,1,0:T(8,128)(2,1)S(1)} %collective-permute-done.4.refs_2_), channel_id=1, source_target_pairs={{0,8},{8,0},{16,24},{24,16},{32,40},{40,32},{48,56},{56,48},{64,72... | collective-permute-start | bytes 2359304 | tf_op jit(solution)/shard_map/ppermute | solution.py:517
  41.2 4.3 %collective-permute-start.9 = (bf16[24,128,128]{2,1,0:T(8,128)(2,1)S(1)}, bf16[24,128,128]{2,1,0:T(8,128)(2,1)S(1)}, u32[]{:S(2)}, u32[]{:S(2)}) collective-permute-start(bf16[24,128,128]{2,1,0:T(8,128)(2,1)S(1)} %collective-permute-done.5.refs_3_), channel_id=1, source_target_pairs={{0,8},{8,0},{16,24},{24,16},{32,40},{40,32},{48,56},{56,48},{64,72... | collective-permute-start | bytes 2359304 | tf_op jit(solution)/shard_map/ppermute | solution.py:517
  43.7 0.9 copy-start.6
  44.7 0.9 copy-start.12
  44.7 1.1 %copy-start.13 = (bf16[24,128,128]{2,1,0:T(8,128)(2,1)}, bf16[24,128,128]{2,1,0:T(8,128)(2,1)S(1)}, u32[]{:S(2)}) copy-start(bf16[24,128,128]{2,1,0:T(8,128)(2,1)S(1)} %collective-permute-done.7.refs_5_) | copy-start | bytes 2359300
  45.5 0.9 copy-start.14
  46.4 0.9 copy-start.15
